TPU v7x, 32 devices: a whole 2x2x4 slice. The times are simulated.
32 devices in a mesh: shard: 8 (over z, x), rep: 4 (over y, core).
Axes of the slice: x: 2, y: 2, z: 4, core: 2. Of those that a mesh axis runs over, the one named last changes fastest.
Arguments:
- tokens: bfloat16 [32, 256, 2048], P(('shard', 'rep')), may hold values from -6 to 6
- segments: int32 [32, 256], P(('shard', 'rep')), may hold values from 0 to 3, never falling along the last dimension, each value on 1 to 128 neighbouring positions
- norm_attn: bfloat16 [2048], P('shard'), may hold values from 0.099609375 to 1.8984375
- w_query: bfloat16 [2048, 2048], P('shard'), may hold values from -0.125 to 0.125
- key_weight: bfloat16 [2048, 512], P('shard'), may hold values from -0.125 to 0.125
- value_weight: bfloat16 [2048, 512], P('shard'), may hold values from -0.125 to 0.125
- w_out: bfloat16 [2048, 2048], P('shard'), may hold values from -0.75 to 0.75
- norm_mlp: bfloat16 [2048], P('shard'), may hold values from 0.099609375 to 1.8984375
- w_gate: bfloat16 [2048, 8192], P('shard'), may hold values from -0.125 to 0.125
- w_up: bfloat16 [2048, 8192], P('shard'), may hold values from -0.125 to 0.125
- w_down: bfloat16 [8192, 2048], P('shard'), may hold values from -0.0625 to 0.0625
- cotangent: float32 [32, 256, 2048], P(('shard', 'rep')), may hold values from -6 to 6
Outputs:
- activations: float32 [32, 256, 2048], P(('shard', 'rep'))
- input_grad: float32 [32, 256, 2048], P(('shard', 'rep'))
- grad_norm_attn: float32 [2048], P('shard')
- grad_query: float32 [2048, 2048], P('shard')
- grad_key: float32 [2048, 512], P('shard')
- grad_value: float32 [2048, 512], P('shard')
- grad_out: float32 [2048, 2048], P('shard')
- grad_norm_mlp: float32 [2048], P('shard')
- grad_gate: float32 [2048, 8192], P('shard')
- grad_up: float32 [2048, 8192], P('shard')
- grad_down: float32 [8192, 2048], P('shard')
Inputs may be any that keep to these rules, and one draw needn't show every extreme that they name: `segments`: segment numbers never fall along a sequence; a document holds 1 to 128 tokens, and one holds exactly 128.
All inputs are finite; a program needn't handle non-finite values.
Results may differ from a plain program's by a relative error of at most 0.02.
Values may be sent and summed in bfloat16 or wider, within the bound.
A program may use at most 512 MiB of HBM per device.

v0:
```python
import functools

import jax
import jax.numpy as jnp
from jax import lax
from jax.experimental import pallas as pl
from jax.experimental.pallas import tpu as pltpu
from jax.sharding import PartitionSpec as P

QUERY_HEADS = 32
KEY_VALUE_HEADS = 8
HEAD_SIZE = 64
GROUP = QUERY_HEADS // KEY_VALUE_HEADS

epsilon = 1e-05
masked_score = -1000000000.0
rope_base = 500000.0
WINDOW = 2
TILE = 256
WIDE_TILE = 512
LOAD_TILE = 128
VMEM_BYTES = 62 * 2**20
BF = jnp.bfloat16
F32 = jnp.float32


def dot(left, right):
    return jnp.dot(left, right, preferred_element_type=F32)


def contract_last(left, right):
    return lax.dot_general(left, right, (((1,), (1,)), ((), ())), preferred_element_type=F32)


def contract_first(left, right):
    return lax.dot_general(left, right, (((0,), (0,)), ((), ())), preferred_element_type=F32)


def positions(segment_ids):
    index = lax.broadcasted_iota(jnp.int32, segment_ids.shape, 1)
    first = jnp.concatenate(
        [
            jnp.ones_like(segment_ids[:, :1]),
            (segment_ids[:, 1:] != segment_ids[:, :-1]).astype(jnp.int32),
        ],
        1,
    )
    starts = lax.cummax(jnp.where(first > 0, index, 0), axis=1)
    return (index - starts).astype(F32)


def rope_tables(segment_ids):
    half = HEAD_SIZE // 2
    inverse = rope_base ** (-(2.0 * jnp.arange(half, dtype=F32)) / HEAD_SIZE)
    angle = positions(segment_ids)[0, :, None] * inverse
    cosine, sine = jnp.cos(angle), jnp.sin(angle)
    return jnp.concatenate([cosine] * 4, 1), jnp.concatenate([-sine, sine] * 2, 1)


def normalize(rows):
    scale_row = lax.rsqrt(jnp.mean(rows * rows, -1, keepdims=True) + epsilon)
    return rows * scale_row, scale_row


def norm_back(grad_unit, unit, scale_row):
    return scale_row * (grad_unit - unit * jnp.mean(grad_unit * unit, -1, keepdims=True))


def rotate(block, cosine, sine):
    lane = lax.broadcasted_iota(jnp.int32, cosine.shape, 1)
    lower = lane % HEAD_SIZE < HEAD_SIZE // 2
    parts = []
    for at in range(0, block.shape[1], 128):
        part = block[:, at : at + 128]
        other = jnp.where(
            lower, pltpu.roll(part, 128 - HEAD_SIZE // 2, 1), pltpu.roll(part, HEAD_SIZE // 2, 1)
        )
        parts.append(part * cosine + other * sine)
    return parts[0] if len(parts) == 1 else jnp.concatenate(parts, 1)


def stack_heads(block, key_head):
    first = key_head * GROUP
    return jnp.concatenate(
        [block[:, (first + i) * HEAD_SIZE : (first + i + 1) * HEAD_SIZE] for i in range(GROUP)], 0
    )


def unstack_heads(rows):
    count = rows.shape[0] // GROUP
    return [rows[i * count : (i + 1) * count] for i in range(GROUP)]


def softmax_rows(query, key, allowed):
    raw = contract_last(query, key) * HEAD_SIZE ** (-0.5)
    scores = jnp.where(allowed, raw, masked_score)
    exponent = jnp.exp(scores - jnp.max(scores, -1, keepdims=True))
    return exponent / jnp.sum(exponent, -1, keepdims=True)


def allowed_rows(seg_column, seg_row):
    count = seg_row.shape[1]
    shape = (count, count)
    causal = lax.broadcasted_iota(jnp.int32, shape, 0) >= lax.broadcasted_iota(jnp.int32, shape, 1)
    one = ((seg_column == seg_row) & causal).astype(jnp.int32)
    return jnp.concatenate([one] * GROUP, 0) > 0


def attend_kernel(q_ref, k_ref, v_ref, cos_ref, sin_ref, segc_ref, segr_ref, qo, ko, vo, ao):
    cosine, sine = cos_ref[...], sin_ref[...]
    allowed = allowed_rows(segc_ref[...], segr_ref[...])
    query = rotate(q_ref[...], cosine, sine).astype(BF)
    key = rotate(k_ref[...], cosine, sine).astype(BF)
    value = v_ref[...].astype(BF)
    qo[...] = query
    ko[...] = key
    vo[...] = value
    heads = []
    for j in range(2):
        cols = slice(j * HEAD_SIZE, (j + 1) * HEAD_SIZE)
        probs = softmax_rows(stack_heads(query, j), key[:, cols], allowed).astype(BF)
        heads += unstack_heads(dot(probs, value[:, cols]).astype(BF))
    ao[...] = jnp.concatenate(heads, 1)


def attend_back_kernel(q_ref, k_ref, v_ref, g_ref, cos_ref, sin_ref, segc_ref, segr_ref, gq, gk, gv):
    cosine, sine = cos_ref[...], -sin_ref[...]
    allowed = allowed_rows(segc_ref[...], segr_ref[...])
    query, key, value, grad = q_ref[...], k_ref[...], v_ref[...], g_ref[...]
    heads, keys, values = [], [], []
    for j in range(2):
        cols = slice(j * HEAD_SIZE, (j + 1) * HEAD_SIZE)
        rows, grad_rows = stack_heads(query, j), stack_heads(grad, j)
        probs = softmax_rows(rows, key[:, cols], allowed)
        grad_probs = contract_last(grad_rows, value[:, cols])
        grad_scores = (
            probs * (grad_probs - jnp.sum(probs * grad_probs, -1, keepdims=True))
        ).astype(BF)
        heads += unstack_heads(dot(grad_scores, key[:, cols]) * HEAD_SIZE ** (-0.5))
        keys.append(contract_first(grad_scores, rows) * HEAD_SIZE ** (-0.5))
        values.append(contract_first(probs.astype(BF), grad_rows))
    gq[...] = rotate(jnp.concatenate(heads, 1), cosine, sine).astype(BF)
    gk[...] = rotate(jnp.concatenate(keys, 1), cosine, sine).astype(BF)
    gv[...] = jnp.concatenate(values, 1).astype(BF)


def attention_specs(count):
    wide = pl.BlockSpec((count, 2 * GROUP * HEAD_SIZE), lambda i: (0, i))
    thin = pl.BlockSpec((count, 2 * HEAD_SIZE), lambda i: (0, i))
    whole = lambda shape: pl.BlockSpec(shape, lambda i: (0, 0))
    fixed = [whole((count, 128)), whole((count, 128)), whole((count, 1)), whole((1, count))]
    return wide, thin, fixed


def attend(query_lin, key_lin, value_lin, tables):
    count = query_lin.shape[0]
    wide, thin, fixed = attention_specs(count)
    kinds = [jax.ShapeDtypeStruct(a.shape, BF) for a in (query_lin, key_lin, value_lin, query_lin)]
    return pl.pallas_call(
        attend_kernel,
        grid=(KEY_VALUE_HEADS // 2,),
        in_specs=[wide, thin, thin] + fixed,
        out_specs=[wide, thin, thin, wide],
        out_shape=kinds,
        compiler_params=pltpu.CompilerParams(vmem_limit_bytes=48 * 2**20),
        cost_estimate=pl.CostEstimate(
            flops=2 * 10**9, bytes_accessed=6 * 10**6, transcendentals=2 * 10**6
        ),
    )(query_lin, key_lin, value_lin, *tables)


def attend_back(query, key, value, grad, tables):
    count = query.shape[0]
    wide, thin, fixed = attention_specs(count)
    kinds = [jax.ShapeDtypeStruct(a.shape, BF) for a in (query, key, value)]
    return pl.pallas_call(
        attend_back_kernel,
        grid=(KEY_VALUE_HEADS // 2,),
        in_specs=[wide, thin, thin, wide] + fixed,
        out_specs=[wide, thin, thin],
        out_shape=kinds,
        compiler_params=pltpu.CompilerParams(vmem_limit_bytes=48 * 2**20),
        cost_estimate=pl.CostEstimate(
            flops=4 * 10**9, bytes_accessed=6 * 10**6, transcendentals=2 * 10**6
        ),
    )(query, key, value, grad, *tables)


def ring_order(count):
    return list(range(0, count, 2)) + list(range(count - 1, 0, -2)) if count % 2 == 0 else list(range(count))


class Ring:
    def __init__(self, count):
        self.count = count
        self.half = count // 2
        self.order = ring_order(count)
        inverse = [self.order.index(i) for i in range(count)]
        self.table = jnp.asarray(self.order, jnp.int32)
        self.turns = []
        self.place = jnp.asarray(inverse, jnp.int32)[lax.axis_index("shard")]

    def at(self, offset):
        return self.table[(self.place + offset + self.count) % self.count]

    def send(self, array, offset):
        n, order = self.count, self.order
        pairs = [(order[i], order[(i + offset) % n]) for i in range(n)]
        return lax.ppermute(array, "shard", pairs)

    def queue(self, *sends):
        arrays = [array for array, _ in sends]
        if len(self.turns) >= WINDOW:
            arrays, _ = lax.optimization_barrier((arrays, self.turns[-WINDOW]))
        got = [self.send(array, offset) for array, (_, offset) in zip(arrays, sends)]
        self.turns.append(got[:2])
        return got

    def gather(self, array):
        cut = array.shape[0] // 2
        ahead = back = array
        out = {0: array}
        for k in range(1, self.half):
            ahead, back = self.queue((ahead, 1), (back, -1))
            out[k], out[-k] = ahead, back
            yield out
        out[self.half] = jnp.concatenate(self.queue((ahead[:cut], 1), (back[cut:], -1)), 0)
        yield out

    def scatter(self, terms):
        (far,) = terms((self.half,))
        far = far.astype(BF)
        cut = far.shape[0] // 2
        ahead, back = self.queue((far[:cut], 1), (far[cut:], -1))
        yield None
        for k in range(self.half - 1, 0, -1):
            up, down = terms((k, -k))
            if k == self.half - 1:
                up = jnp.concatenate([up[:cut] + ahead.astype(F32), up[cut:]], 0)
                down = jnp.concatenate([down[:cut], down[cut:] + back.astype(F32)], 0)
            else:
                up, down = up + ahead.astype(F32), down + back.astype(F32)
            ahead, back = self.queue((up.astype(BF), 1), (down.astype(BF), -1))
            if k > 1:
                yield None
        (own,) = terms((0,))
        yield own + ahead.astype(F32) + back.astype(F32)


def run(*flows):
    flows = list(flows)
    last = [None] * len(flows)
    live = list(range(len(flows)))
    while live:
        for i in list(live):
            try:
                last[i] = next(flows[i])
            except StopIteration:
                live.remove(i)
    return last


def ring_place(count, shard):
    return jnp.where(shard % 2 == 0, shard // 2, count - 1 - shard // 2)


def ring_shard(count, place):
    place = (place + count) % count
    return jnp.where(place < count // 2, 2 * place, 2 * (count - 1 - place) + 1)


def core_partner(rep):
    return rep + 1 - 2 * (rep % 2)


def chip_partner(rep):
    return (rep + 2) % 4


def greet(devices):
    barrier = pltpu.get_barrier_semaphore()
    for device in devices:
        pl.semaphore_signal(
            barrier, inc=1, device_id=device, device_id_type=pl.DeviceIdType.MESH
        )
    pl.semaphore_wait(barrier, len(devices))


def remote_copy(src, dst, send, recv, device):
    return pltpu.make_async_remote_copy(
        src_ref=src,
        dst_ref=dst,
        send_sem=send,
        recv_sem=recv,
        device_id=device,
        device_id_type=pl.DeviceIdType.MESH,
    )


def front_kernel(
    count,
    tokens_ref,
    gains_ref,
    cotangent_ref,
    cos_ref,
    sin_ref,
    segc_ref,
    segr_ref,
    query_own_ref,
    key_own_ref,
    value_own_ref,
    out_own_ref,
    gate_ref,
    up_ref,
    qkv_all_ref,
    out_all_ref,
    both_ref,
    low_all_ref,
    gains_all_ref,
    query_ref,
    key_ref,
    value_ref,
    attended_ref,
    middle_ref,
    normed_two_ref,
    low_own,
    both_own,
    qkv_all,
    out_all,
    normed,
    linear,
    own_sem,
    load_sem,
    gain_send,
    gain_recv,
    ring_send,
    ring_recv,
    core_send,
    core_recv,
    chip_send,
    chip_recv,
    across_send,
    across_recv,
    group_send,
    group_recv,
    low_send,
    low_recv,
):
    half = count // 2
    me, rep = lax.axis_index("shard"), lax.axis_index("rep")
    core, chip = rep % 2, rep // 2
    place = ring_place(count, me)
    others = [ring_shard(count, place + k) for k in range(1, count)]
    near = ({"shard": ring_shard(count, place + 1)}, {"shard": ring_shard(count, place - 1)})
    other_core, other_chip = {"rep": core_partner(rep)}, {"rep": chip_partner(rep)}
    own_rows = query_own_ref.shape[0]
    quarter = own_rows // 4
    cut = quarter // 2
    ff_own = gate_ref.shape[1] // count
    rows, width = tokens_ref.shape
    full_refs = (qkv_all_ref, out_all_ref)
    inside = (qkv_all, out_all)

    def rows_at(start, size):
        return pl.ds(pl.multiple_of(start, cut), size)

    def shard_rows(shard):
        return rows_at(shard * own_rows, own_rows)

    def piece_of(shard, which_core, which_chip, part=None):
        start = shard * own_rows + (2 * which_core + which_chip) * quarter
        if part is None:
            return rows_at(start, quarter)
        return rows_at(start + part * cut, cut)

    own_loads = [
        pltpu.make_async_copy(out_own_ref, out_all.at[shard_rows(me)], own_sem.at[6])
    ]
    start = 0
    for index, ref in enumerate((query_own_ref, key_own_ref, value_own_ref)):
        columns = pl.ds(start, ref.shape[1])
        own_loads.append(
            pltpu.make_async_copy(ref, qkv_all.at[shard_rows(me), columns], own_sem.at[7 + index])
        )
        start += ref.shape[1]
    keep = [
        pltpu.make_async_copy(
            inside[i].at[shard_rows(me)], full_refs[i].at[shard_rows(me)], own_sem.at[i]
        )
        for i in range(2)
    ]
    for i, ref in enumerate((gate_ref, up_ref)):
        block = (rows_at(rep * quarter, quarter), pl.ds(pl.multiple_of(me * ff_own, 128), ff_own))
        own_loads.append(
            pltpu.make_async_copy(
                ref.at[block], both_own.at[:, pl.ds(i * ff_own, ff_own)], own_sem.at[2 + i]
            )
        )
    for copy in own_loads:
        copy.start()
    gains_all_ref[:, pl.ds(pl.multiple_of(me * own_rows, 128), own_rows)] = gains_ref[...]
    low_own[...] = cotangent_ref[...].astype(BF)
    for copy in own_loads:
        copy.wait()
    keep.append(pltpu.make_async_copy(low_own, low_all_ref.at[pl.ds(0, rows)], own_sem.at[4]))
    keep.append(pltpu.make_async_copy(both_own, both_ref.at[me, rep], own_sem.at[5]))
    for copy in keep:
        copy.start()

    greet([{"shard": shard} for shard in others] + [other_core, other_chip])

    def gain_copy(k):
        columns = pl.ds(pl.multiple_of(me * own_rows, 128), own_rows)
        return remote_copy(
            gains_ref,
            gains_all_ref.at[:, columns],
            gain_send.at[k - 1],
            gain_recv.at[k - 1],
            {"shard": others[k - 1]},
        )

    def across(k, which):
        ref = (gate_ref, up_ref)[which]
        there = others[k - 1]
        columns = pl.ds(pl.multiple_of(there * ff_own, 128), ff_own)
        return remote_copy(
            ref.at[rows_at(rep * quarter, quarter), columns],
            both_ref.at[me, rep, :, pl.ds(which * ff_own, ff_own)],
            across_send.at[which, k - 1],
            across_recv.at[which, k - 1],
            {"shard": there},
        )

    def ring_copy(i, direction, step):
        sign = 1 if direction == 0 else -1
        shard = ring_shard(count, place - sign * (step - 1))
        if step < half:
            at = piece_of(shard, core, chip)
        else:
            at = piece_of(shard, core, chip, direction)
        src = full_refs[i].at[at]
        if step == 1:
            src = inside[i].at[at]
        return remote_copy(
            src,
            full_refs[i].at[at],
            ring_send.at[i, direction, step - 1],
            ring_recv.at[i, direction, step - 1],
            near[direction],
        )

    def chip_copy(i, k):
        at = piece_of(ring_shard(count, place - k), core, chip)
        slot = k + half - 1
        return remote_copy(
            full_refs[i].at[at],
            full_refs[i].at[at],
            chip_send.at[i, slot],
            chip_recv.at[i, slot],
            other_chip,
        )

    def core_copy(i, k, which):
        from_chip = chip if which == 0 else 1 - chip
        at = piece_of(ring_shard(count, place - k), core, from_chip)
        slot = k + half - 1
        return remote_copy(
            full_refs[i].at[at],
            full_refs[i].at[at],
            core_send.at[i, which, slot],
            core_recv.at[i, which, slot],
            other_core,
        )

    def load(i, k):
        at = shard_rows(ring_shard(count, place - k))
        return pltpu.make_async_copy(
            full_refs[i].at[at], inside[i].at[at], load_sem.at[i, k + half - 1]
        )

    def low_copy(direction, step):
        base = 0 if direction == 0 else half
        to, size = (base + step) * rows, rows
        source = to - rows
        if step == half:
            size = rows // 2
            to = half * rows + direction * size
            source = (base + half - 1) * rows + direction * size
        src = low_all_ref.at[pl.ds(source, size)] if step > 1 else low_own
        return remote_copy(
            src,
            low_all_ref.at[pl.ds(to, size)],
            low_send.at[direction, step - 1],
            low_recv.at[direction, step - 1],
            near[direction],
        )

    def start_low(step):
        for direction in range(2):
            low_copy(direction, step).start()

    def finish_low(step):
        for direction in range(2):
            low_copy(direction, step).wait_recv()
        if step < half:
            start_low(step + 1)

    def start_step(i, step):
        for direction in range(2):
            ring_copy(i, direction, step).start()

    def places(step):
        return (step, -step) if step < half else (half,)

    def finish_step(i, step):
        for direction in range(2):
            ring_copy(i, direction, step).wait_recv()
        if step < half:
            start_step(i, step + 1)
        for k in places(step):
            core_copy(i, k, 0).start()

    def start_chip(i, step):
        for k in places(step):
            chip_copy(i, k).start()

    def pass_step(i, step):
        for k in places(step):
            chip_copy(i, k).wait_recv()
            core_copy(i, k, 1).start()

    def load_step(i, step):
        for k in places(step):
            for which in range(2):
                core_copy(i, k, which).wait_recv()
            load(i, k).start()

    for k in range(1, count):
        gain_copy(k).start()
    start_step(0, 1)
    resid = tokens_ref[...].astype(F32)
    unit, _ = normalize(resid)
    for k in range(1, count):
        gain_copy(k).wait_recv()
    normed[...] = (unit * gains_all_ref[0:1, :]).astype(BF)

    for step in range(1, half + 1):
        finish_step(0, step)
        start_chip(0, step)
        if step == half - 1:
            for k in range(1, count):
                for which in range(2):
                    across(k, which).start()
    start_step(1, 1)
    for step in range(1, half + 1):
        pass_step(0, step)
        if step > 1:
            load_step(0, step - 1)

    def group_copy(index, quarter_at, device):
        at = both_ref.at[:, quarter_at]
        return remote_copy(at, at, group_send.at[index], group_recv.at[index], device)

    chip_copies = [group_copy(0, rep, other_chip)]
    core_copies = [
        group_copy(1, rep, other_core),
        group_copy(2, chip_partner(rep), other_core),
    ]
    load_step(0, half)
    for k in range(-(half - 1), half + 1):
        if k:
            load(0, k).wait()

    def linear_tile(j, carry):
        at = pl.ds(pl.multiple_of(j * TILE, TILE), TILE)
        linear[:, at] = dot(normed[...], qkv_all[:, at])
        return carry

    lax.fori_loop(0, linear.shape[1] // TILE, linear_tile, 0)

    cosine, sine = cos_ref[...], sin_ref[...]
    wide, thin = 2 * GROUP * HEAD_SIZE, 2 * HEAD_SIZE
    key_at, value_at = width, width + key_ref.shape[1]

    def heads_pair(pair):
        allowed = allowed_rows(segc_ref[...], segr_ref[...])
        wide_at = pl.ds(pair * wide, wide)
        thin_at = pl.ds(pair * thin, thin)
        query = rotate(linear[:, wide_at], cosine, sine).astype(BF)
        key = rotate(linear[:, pl.ds(key_at + pair * thin, thin)], cosine, sine).astype(BF)
        value = linear[:, pl.ds(value_at + pair * thin, thin)].astype(BF)
        query_ref[:, wide_at] = query
        key_ref[:, thin_at] = key
        value_ref[:, thin_at] = value
        heads = []
        for j in range(2):
            cols = slice(j * HEAD_SIZE, (j + 1) * HEAD_SIZE)
            probs = softmax_rows(stack_heads(query, j), key[:, cols], allowed).astype(BF)
            heads += unstack_heads(dot(probs, value[:, cols]).astype(BF))
        attended_ref[:, wide_at] = jnp.concatenate(heads, 1)

    pairs = KEY_VALUE_HEADS // 2
    for turn in range(max(pairs, half)):
        if turn < half:
            finish_step(1, turn + 1)
            start_chip(1, turn + 1)
        if turn == half - 2:
            start_low(1)
        if turn < pairs:
            heads_pair(turn)
    for copy in keep:
        copy.wait()
    for k in range(1, count):
        for which in range(2):
            across(k, which).wait_recv()
    chip_copies[0].start()
    core_copies[0].start()
    for step in range(1, half + 1):
        pass_step(1, step)
        if step > 1:
            load_step(1, step - 1)
        if step % 2 == 0 and step // 2 < half:
            finish_low(step // 2)
    load_step(1, half)
    for k in range(-(half - 1), half + 1):
        if k:
            load(1, k).wait()

    def branch_tile(j, carry):
        at = pl.ds(pl.multiple_of(j * TILE, TILE), TILE)
        branch = dot(attended_ref[...], out_all[:, at])
        middle_ref[:, at] = tokens_ref[:, at].astype(F32) + branch
        return carry

    lax.fori_loop(0, width // TILE, branch_tile, 0)
    unit, _ = normalize(middle_ref[...])
    normed_two_ref[...] = (unit * gains_all_ref[1:2, :]).astype(BF)

    for step in range(half // 2 + 1, half + 1):
        finish_low(step)
    chip_copies[0].wait_recv()
    core_copies[1].start()
    for copy in core_copies:
        copy.wait_recv()
    for copy in chip_copies + core_copies:
        copy.wait_send()
    for step in range(1, half + 1):
        for direction in range(2):
            low_copy(direction, step).wait_send()
    for i in range(2):
        for step in range(1, half + 1):
            for direction in range(2):
                ring_copy(i, direction, step).wait_send()
            for k in places(step):
                chip_copy(i, k).wait_send()
                for which in range(2):
                    core_copy(i, k, which).wait_send()
    for k in range(1, count):
        gain_copy(k).wait_send()
        for which in range(2):
            across(k, which).wait_send()


def front(count, tokens, gains, cotangent, tables, own, gate_own, up_own):
    rows, width = tokens.shape
    own_rows, wide_k = own[1].shape
    qkv_width = width + 2 * wide_k
    ff_own = gate_own.shape[1] // count
    half = count // 2
    here = pl.BlockSpec(memory_space=pl.ANY)
    inside = pl.BlockSpec(memory_space=pltpu.VMEM)
    kind = jax.ShapeDtypeStruct
    dma = pltpu.SemaphoreType.DMA
    return pl.pallas_call(
        functools.partial(front_kernel, count),
        in_specs=[inside] * 7 + [here] * 6,
        out_specs=[here] * 4 + [inside] * 7,
        out_shape=[
            kind((count * own_rows, qkv_width), BF),
            kind((count * own_rows, width), BF),
            kind((count, 4, own_rows // 4, 2 * ff_own), BF),
            kind((count * rows, width), BF),
            kind((gains.shape[0], width), F32),
            kind((rows, width), BF),
            kind((rows, wide_k), BF),
            kind((rows, wide_k), BF),
            kind((rows, width), BF),
            kind((rows, width), F32),
            kind((rows, width), BF),
        ],
        scratch_shapes=[
            pltpu.VMEM((rows, width), BF),
            pltpu.VMEM((own_rows // 4, 2 * ff_own), BF),
            pltpu.VMEM((count * own_rows, qkv_width), BF),
            pltpu.VMEM((count * own_rows, width), BF),
            pltpu.VMEM((rows, width), BF),
            pltpu.VMEM((rows, qkv_width), F32),
            dma((10,)),
            dma((2, count)),
            dma((count - 1,)),
            dma((count - 1,)),
            dma((2, 2, half)),
            dma((2, 2, half)),
            dma((2, 2, count)),
            dma((2, 2, count)),
            dma((2, count)),
            dma((2, count)),
            dma((2, count - 1)),
            dma((2, count - 1)),
            dma((3,)),
            dma((3,)),
            dma((2, half)),
            dma((2, half)),
        ],
        compiler_params=pltpu.CompilerParams(
            collective_id=1, has_side_effects=True, vmem_limit_bytes=VMEM_BYTES
        ),
        cost_estimate=pl.CostEstimate(
            flops=2 * rows * width * (qkv_width + width) + 2 * 10**9,
            bytes_accessed=60 * 10**6,
            transcendentals=2 * 10**6,
        ),
    )(tokens, gains, cotangent, *tables, *own, gate_own, up_own)


def feed_forward_kernel(
    count,
    normed_ref,
    low_ref,
    both_ref,
    down_ref,
    grad_ref,
    branch_ref,
    sums_ref,
    down_grad_ref,
    normed,
    low,
    hidden,
    grads,
    w_both,
    w_down,
    turned,
    staged,
    from_core,
    core_sums,
    from_chip,
    group_sums,
    result_tile,
    outgoing,
    incoming,
    local_sem,
    gather_send,
    gather_recv,
    scatter_send,
    scatter_recv,
    credit,
    core_send,
    core_recv,
    chip_send,
    chip_recv,
    group_credit,
    sums_sem,
    result_sem,
    down_send,
    down_recv,
):
    half = count // 2
    rows = normed_ref.shape[0]
    cut = rows // 2
    width = normed_ref.shape[1]
    ff = down_ref.shape[0]
    place = ring_place(count, lax.axis_index("shard"))
    neighbours = (ring_shard(count, place + 1), ring_shard(count, place - 1))
    rep = lax.axis_index("rep")
    core, chip = rep % 2, rep // 2
    other_core, other_chip = {"rep": core_partner(rep)}, {"rep": chip_partner(rep)}
    everywhere = pl.ds(0, rows)
    halves = (pl.ds(0, cut), pl.ds(cut, cut))

    def at(slot, part=None):
        start, size = (0, rows) if part is None else (part * cut, cut)
        return pl.ds(pl.multiple_of(slot * rows + start, cut), size)

    def tile(j):
        return pl.ds(pl.multiple_of(j * TILE, TILE), TILE)

    def remote(src, dst, send, recv, direction):
        return remote_copy(src, dst, send, recv, {"shard": neighbours[direction]})

    loads = [
        pltpu.make_async_copy(normed_ref, normed.at[at(0)], local_sem.at[0]),
        pltpu.make_async_copy(low_ref, low, local_sem.at[1]),
        pltpu.make_async_copy(both_ref, w_both, local_sem.at[2]),
        pltpu.make_async_copy(down_ref, w_down, local_sem.at[3]),
    ]
    for load in loads:
        load.start()

    for chain in range(2):
        for direction in range(2):
            blank = halves[1 - direction]
            incoming[chain, direction, 0, blank] = jnp.zeros((cut, width), BF)

    greet([{"shard": neighbour} for neighbour in neighbours] + [other_core, other_chip])

    def gathered(part, direction, step):
        base = 0 if direction == 0 else half
        if isinstance(step, int) and step == 1:
            source = 0
        else:
            source = jnp.where(step == 1, 0, base + step - 1)
        return remote(
            normed.at[at(source, part)],
            normed.at[at(base + step, part)],
            gather_send.at[part, direction, step - 1],
            gather_recv.at[part, direction, step - 1],
            direction,
        )

    def gathered_last(direction):
        source = half - 1 if direction == 0 else 2 * half - 1
        return remote(
            normed.at[at(source, direction)],
            normed.at[at(half, direction)],
            gather_send.at[0, direction, half - 1],
            gather_recv.at[0, direction, half - 1],
            direction,
        )

    def products(slot):
        mine = at(slot)

        def body(j, carry):
            gate_at, up_at = tile(j), tile(j + ff // TILE)
            own = normed[mine, :]
            gate = dot(own, w_both[:, gate_at])
            up = dot(own, w_both[:, up_at])
            grad_hidden = contract_last(low[mine, :], w_down[gate_at, :])
            sigmoid = jax.nn.sigmoid(gate)
            silu = gate * sigmoid
            hidden[mine, gate_at] = (silu * up).astype(BF)
            grads[mine, gate_at] = (
                grad_hidden * up * sigmoid * (1.0 + gate * (1.0 - sigmoid))
            ).astype(BF)
            grads[mine, up_at] = (grad_hidden * silu).astype(BF)
            return carry

        lax.fori_loop(0, ff // TILE, body, 0)

    both_ways = ((0, 0), (0, 1), (1, 0), (1, 1))
    loads[0].wait()
    for part, direction in both_ways:
        gathered(part, direction, 1).start()
    for load in loads[1:]:
        load.wait()
    products(0)

    def gather_step(step, carry):
        for part, direction in both_ways:
            gathered(part, direction, step).wait_recv()

            @pl.when(step < half - 1)
            def _():
                gathered(part, direction, step + 1).start()

            if part == direction:

                @pl.when(step == half - 1)
                def _():
                    gathered_last(direction).start()

        products(step)

        @pl.when(step < half - 1)
        def _():
            products(half + step)

        return carry

    lax.fori_loop(1, half, gather_step, 0)
    for direction in range(2):
        gathered_last(direction).wait_recv()
    products(half)

    def term(chain, rows_at, j):
        if chain == 0:
            return contract_last(grads[rows_at, :], w_both[tile(j), :])
        return dot(hidden[rows_at, :], w_down[:, tile(j)])

    def scattered(chain, direction, step):
        if isinstance(step, int) and step == 0:
            own, there = halves[direction], 0
        else:
            own, there = everywhere, step % 2
        return remote(
            outgoing.at[chain, direction, own],
            incoming.at[chain, direction, there, own],
            scatter_send.at[chain, direction, step],
            scatter_recv.at[chain, direction, step],
            direction,
        )

    units = (width + ff) // TILE
    per_step = -(-(units + 3) // (half - 1))
    quarter = TILE // 4

    def core_copy(unit):
        spot = unit % 2
        return remote_copy(
            staged.at[spot, :, 1 - core],
            from_core.at[spot],
            core_send.at[spot],
            core_recv.at[spot],
            other_core,
        )

    def chip_copy(unit):
        spot = unit % 3
        return remote_copy(
            core_sums.at[spot, 1 - chip],
            from_chip.at[spot],
            chip_send.at[spot],
            chip_recv.at[spot],
            other_chip,
        )

    down_units = ff // TILE

    def sums_copy(unit, down):
        spot = unit % 2
        target = down_grad_ref.at[unit, rep] if down else sums_ref.at[unit - down_units]
        return pltpu.make_async_copy(group_sums.at[spot], target, sums_sem.at[spot])

    def for_sums(unit, act):
        @pl.when(unit < down_units)
        def _():
            act(sums_copy(unit, True))

        @pl.when(unit >= down_units)
        def _():
            act(sums_copy(unit, False))

    def down_copy(index):
        at = down_grad_ref.at[:, chip_partner(rep) if index == 2 else rep]
        return remote_copy(
            at,
            at,
            down_send.at[index],
            down_recv.at[index],
            other_chip if index == 0 else other_core,
        )

    def give_credit(which, device):
        pl.semaphore_signal(
            group_credit.at[which], inc=1, device_id=device, device_id_type=pl.DeviceIdType.MESH
        )

    def weight_unit(unit):
        spot = unit % 2

        def from_arrays(left, right, block):
            def turn(c, carry):
                turned[:, at(c)] = left[at(c), tile(block)].T
                return carry

            lax.fori_loop(0, count, turn, 0)

            def body(j, carry):
                value = dot(turned[...], right[:, tile(j)]).astype(BF)
                staged[spot, :, :, :, tile(j)] = value.reshape(2, 2, quarter, TILE)
                return carry

            lax.fori_loop(0, width // TILE, body, 0)

        @pl.when(unit < down_units)
        def _():
            from_arrays(hidden, low, unit)

        @pl.when(unit >= down_units)
        def _():
            from_arrays(normed, grads, unit - down_units)

        @pl.when(unit >= 2)
        def _():
            pl.semaphore_wait(group_credit.at[0], 1)

        core_copy(unit).start()

    def sum_over_cores(unit):
        spot, place_of = unit % 2, unit % 3
        core_copy(unit).wait()
        for y in range(2):
            total = staged[spot, y, core].astype(F32) + from_core[spot, y].astype(F32)
            core_sums[place_of, y] = total.astype(BF)

        @pl.when(unit < units - 2)
        def _():
            give_credit(0, other_core)

        @pl.when(unit >= 3)
        def _():
            pl.semaphore_wait(group_credit.at[1], 1)

        chip_copy(unit).start()

    def sum_over_chips(unit):
        spot, place_of = unit % 2, unit % 3
        chip_copy(unit).wait()

        @pl.when(unit >= 2)
        def _():
            for_sums(unit - 2, lambda copy: copy.wait())

        total = core_sums[place_of, chip].astype(F32) + from_chip[place_of].astype(F32)
        group_sums[spot] = total.astype(BF)

        @pl.when(unit < units - 3)
        def _():
            give_credit(1, other_chip)

        for_sums(unit, lambda copy: copy.start())

    def weight_step(turn):
        @pl.when(turn < units)
        def _():
            weight_unit(turn)

        @pl.when((turn >= 1) & (turn <= units))
        def _():
            sum_over_cores(turn - 1)

        @pl.when(turn == units)
        def _():
            for index in range(2):
                down_copy(index).start()

        @pl.when(turn >= 3)
        def _():
            sum_over_chips(turn - 3)

    for chain in range(2):

        def first(j, carry):
            value = term(chain, at(half), j).astype(BF)
            outgoing[chain, 0, halves[0], tile(j)] = value[:cut]
            outgoing[chain, 1, halves[1], tile(j)] = value[cut:]
            return carry

        lax.fori_loop(0, width // TILE, first, 0)
        for direction in range(2):
            scattered(chain, direction, 0).start()

    products(2 * half - 1)

    def scatter_step(step, carry):
        k = half - step
        for chain in range(2):
            for direction in range(2):
                slot = half + k if direction == 0 else k

                @pl.when(step == 1)
                def _():
                    scattered(chain, direction, 0).wait()

                @pl.when(step > 1)
                def _():
                    scattered(chain, direction, step - 1).wait()
                    pl.semaphore_wait(credit.at[chain, direction], 1)

                def add(j, carry):
                    value = term(chain, at(slot), j)
                    value += incoming[chain, direction, (step - 1) % 2, :, tile(j)].astype(F32)
                    outgoing[chain, direction, :, tile(j)] = value.astype(BF)
                    return carry

                lax.fori_loop(0, width // TILE, add, 0)
                scattered(chain, direction, step).start()

                @pl.when(step < half - 1)
                def _():
                    pl.semaphore_signal(
                        credit.at[chain, direction],
                        inc=1,
                        device_id={"shard": neighbours[1 - direction]},
                        device_id_type=pl.DeviceIdType.MESH,
                    )

        lax.fori_loop(
            (step - 1) * per_step,
            jnp.minimum(step * per_step, units + 3),
            lambda turn, c: (weight_step(turn), c)[1],
            0,
        )
        return carry

    lax.fori_loop(1, half, scatter_step, 0)

    for chain, result in enumerate((grad_ref, branch_ref)):
        for direction in range(2):
            scattered(chain, direction, half - 1).wait()

        def result_copy(j):
            return pltpu.make_async_copy(
                result_tile.at[j % 2], result.at[:, tile(j)], result_sem.at[j % 2]
            )

        def last(j, carry):
            @pl.when(j >= 2)
            def _():
                result_copy(j - 2).wait()

            value = term(chain, at(0), j)
            for direction in range(2):
                value += incoming[chain, direction, (half - 1) % 2, :, tile(j)].astype(F32)
            result_tile[j % 2] = value
            result_copy(j).start()
            return carry

        lax.fori_loop(0, width // TILE, last, 0)
        for j in (width // TILE - 2, width // TILE - 1):
            result_copy(j).wait()

    down_copy(0).wait_recv()
    down_copy(2).start()
    for unit in (units - 2, units - 1):
        sums_copy(unit, False).wait()
    down_copy(0).wait_send()
    for index in (1, 2):
        down_copy(index).wait()
    for part, direction in both_ways:
        lax.fori_loop(
            1,
            half,
            lambda step, c: (gathered(part, direction, step).wait_send(), c)[1],
            0,
        )
    for direction in range(2):
        gathered_last(direction).wait_send()


def feed_forward_bytes(count, rows, width, ff):
    tokens = count * rows
    return 2 * (
        tokens * (2 * width + 3 * ff)
        + 3 * width * ff
        + TILE * tokens
        + 6 * TILE * width
        + 12 * rows * width
        + 4 * TILE * rows
    )


def feed_forward(count, normed, low, w_both, w_down):
    rows, width = normed.shape
    ff = w_down.shape[0]
    tokens = count * rows
    half = count // 2
    quarter = TILE // 4
    here = pl.BlockSpec(memory_space=pl.ANY)
    dma = pltpu.SemaphoreType.DMA
    return pl.pallas_call(
        functools.partial(feed_forward_kernel, count),
        in_specs=[here] * 4,
        out_specs=[here] * 4,
        out_shape=[
            jax.ShapeDtypeStruct((rows, width), F32),
            jax.ShapeDtypeStruct((rows, width), F32),
            jax.ShapeDtypeStruct((width // TILE, quarter, width), BF),
            jax.ShapeDtypeStruct((ff // TILE, 4, quarter, width), BF),
        ],
        scratch_shapes=[
            pltpu.VMEM((tokens, width), BF),
            pltpu.VMEM((tokens, width), BF),
            pltpu.VMEM((tokens, ff), BF),
            pltpu.VMEM((tokens, 2 * ff), BF),
            pltpu.VMEM((width, 2 * ff), BF),
            pltpu.VMEM((ff, width), BF),
            pltpu.VMEM((TILE, tokens), BF),
            pltpu.VMEM((2, 2, 2, quarter, width), BF),
            pltpu.VMEM((2, 2, quarter, width), BF),
            pltpu.VMEM((3, 2, quarter, width), BF),
            pltpu.VMEM((3, quarter, width), BF),
            pltpu.VMEM((2, quarter, width), BF),
            pltpu.VMEM((2, rows, TILE), F32),
            pltpu.VMEM((2, 2, rows, width), BF),
            pltpu.VMEM((2, 2, 2, rows, width), BF),
            dma((4,)),
            dma((2, 2, half)),
            dma((2, 2, half)),
            dma((2, 2, half)),
            dma((2, 2, half)),
            pltpu.SemaphoreType.REGULAR((2, 2)),
            dma((2,)),
            dma((2,)),
            dma((3,)),
            dma((3,)),
            pltpu.SemaphoreType.REGULAR((2,)),
            dma((2,)),
            dma((2,)),
            dma((3,)),
            dma((3,)),
        ],
        compiler_params=pltpu.CompilerParams(
            collective_id=0, has_side_effects=True, vmem_limit_bytes=VMEM_BYTES
        ),
        cost_estimate=pl.CostEstimate(
            flops=18 * tokens * width * ff, bytes_accessed=50 * 10**6, transcendentals=tokens * ff
        ),
    )(normed, low, w_both, w_down)


def middle_back_kernel(middle_ref, grad_ref, cotangent_ref, gain_ref, out_ref, low_ref, term_ref):
    unit, scale_row = normalize(middle_ref[...])
    grad = grad_ref[...]
    total = cotangent_ref[...] + norm_back(grad * gain_ref[...], unit, scale_row)
    out_ref[...] = total
    low_ref[...] = total.astype(BF)
    term = jnp.sum(grad * unit, 0, keepdims=True)

    @pl.when(pl.program_id(0) == 0)
    def _():
        term_ref[...] = term

    @pl.when(pl.program_id(0) > 0)
    def _():
        term_ref[...] += term


def middle_back(middle, grad, cotangent, gain):
    rows, width = middle.shape
    block = pl.BlockSpec((rows // 8, width), lambda i: (i, 0))
    fixed = pl.BlockSpec((1, width), lambda i: (0, 0))
    kind = jax.ShapeDtypeStruct
    return pl.pallas_call(
        middle_back_kernel,
        grid=(8,),
        in_specs=[block, block, block, fixed],
        out_specs=[block, block, fixed],
        out_shape=[kind((rows, width), F32), kind((rows, width), BF), kind((1, width), F32)],
    )(middle, grad, cotangent, gain)


def back_kernel(
    count,
    sums_ref,
    mid_low_ref,
    gain_two_ref,
    attended_ref,
    query_ref,
    key_ref,
    value_ref,
    tokens_ref,
    gains_ref,
    cos_ref,
    sin_ref,
    segc_ref,
    segr_ref,
    qkv_all_ref,
    out_all_ref,
    gate_grad_ref,
    up_grad_ref,
    out_grad_ref,
    qkv_grad_ref,
    grad_input_ref,
    gain_grad_ref,
    both_own,
    turned,
    grad_attended,
    grads,
    weight_tile,
    terms_first,
    terms_second,
    from_core_out,
    from_core_qkv,
    from_chip_out,
    out_sums,
    out_summed,
    outgoing_out,
    outgoing_qkv,
    incoming_out,
    incoming_qkv,
    summed,
    from_chip,
    finished,
    gain_terms,
    gains_in,
    gain_parts,
    gain_swaps,
    own_sem,
    tile_sem,
    across_send,
    across_recv,
    group_send,
    group_recv,
    core_send,
    core_recv,
    ring_send,
    ring_recv,
    chip_send,
    chip_recv,
    last_send,
    last_recv,
    pair_send,
    pair_recv,
    gain_send,
    gain_recv,
    swap_send,
    swap_recv,
):
    half = count // 2
    me, rep = lax.axis_index("shard"), lax.axis_index("rep")
    core, chip = rep % 2, rep // 2
    place = ring_place(count, me)
    others = [ring_shard(count, place + k) for k in range(1, count)]
    near = ({"shard": ring_shard(count, place + 1)}, {"shard": ring_shard(count, place - 1)})
    other_core, other_chip = {"rep": core_partner(rep)}, {"rep": chip_partner(rep)}
    rows, width = tokens_ref.shape
    own_rows = width // count
    strip, quarter = own_rows // 2, own_rows // 4
    ff_own = gate_grad_ref.shape[2] // count
    qkv_half = grads.shape[1] // 2
    wides = (width, qkv_half, qkv_half)
    terms = (terms_first, terms_second, terms_first)
    pieces = (quarter, strip, strip)
    from_core = (from_core_out, from_core_qkv.at[0], from_core_qkv.at[1])
    outgoing = (outgoing_out, outgoing_qkv.at[0], outgoing_qkv.at[1])
    incoming = (incoming_out, incoming_qkv.at[0], incoming_qkv.at[1])
    result_refs = (out_grad_ref, qkv_grad_ref, qkv_grad_ref)
    result_starts = (0, 0, qkv_half)
    chains, in_turn = range(3), (1, 2, 0)

    def tile(j, size=TILE):
        return pl.ds(pl.multiple_of(j * size, size), size)

    gate_up = (gate_grad_ref, up_grad_ref)

    def own_columns(shard):
        return pl.ds(pl.multiple_of(shard * ff_own, 128), ff_own)

    def across(k, which):
        there = others[k - 1]
        return remote_copy(
            sums_ref.at[there, :, pl.ds(which * ff_own, ff_own)],
            gate_up[which].at[rep, :, own_columns(me)],
            across_send.at[which, k - 1],
            across_recv.at[which, k - 1],
            {"shard": there},
        )

    own_load = pltpu.make_async_copy(sums_ref.at[me], both_own, own_sem.at[0])
    keep = [
        pltpu.make_async_copy(
            both_own.at[:, pl.ds(which * ff_own, ff_own)],
            gate_up[which].at[rep, :, own_columns(me)],
            own_sem.at[which],
        )
        for which in range(2)
    ]

    def group_copy(which, index):
        member = chip_partner(rep) if index == 2 else rep
        dst = src = gate_up[which].at[member]
        return remote_copy(
            src,
            dst,
            group_send.at[which, index],
            group_recv.at[which, index],
            other_chip if index == 0 else other_core,
        )

    def shard_of(k):
        return ring_shard(count, place + k)

    def core_copy(i, k):
        slot = k + half - 1
        return remote_copy(
            terms[i].at[shard_of(k), 1 - core, :, pl.ds(0, wides[i])],
            from_core[i].at[slot],
            core_send.at[i, slot],
            core_recv.at[i, slot],
            other_core,
        )

    def all_terms(i):
        def body(j, carry):
            if i == 0:
                right = mid_low_ref[:, tile(j)]
            else:
                right = grads[:, tile(j + result_starts[i] // TILE)]
            value = dot(turned[...], right).astype(BF)
            terms[i][:, :, :, tile(j)] = value.reshape(count, 2, strip, TILE)
            return carry

        lax.fori_loop(0, wides[i] // TILE, body, 0)
        for k in [half] + [s * j for j in range(half - 1, 0, -1) for s in (1, -1)] + [0]:
            core_copy(i, k).start()

    def pair_copy(k):
        slot = k + half - 1
        return remote_copy(
            out_sums.at[slot, 1 - chip],
            from_chip_out.at[slot],
            pair_send.at[slot],
            pair_recv.at[slot],
            other_chip,
        )

    def sum_pair(k):
        core_copy(0, k).wait_recv()

        def body(j, carry):
            at = tile(j, WIDE_TILE)
            value = terms[0][shard_of(k), core, :, at].astype(F32)
            value += from_core[0][k + half - 1, :, at].astype(F32)
            out_sums[k + half - 1, :, :, at] = value.astype(BF).reshape(2, quarter, WIDE_TILE)
            return carry

        lax.fori_loop(0, wides[0] // WIDE_TILE, body, 0)
        pair_copy(k).start()

    def piece_sum(i, k, extra, store):
        slot = k + half - 1
        if i == 0:
            pair_copy(k).wait_recv()
            received = from_chip_out
        else:
            core_copy(i, k).wait_recv()
            received = from_core[i]

        def body(j, carry):
            at = tile(j, WIDE_TILE)
            own = out_sums[slot, chip, :, at] if i == 0 else terms[i][shard_of(k), core, :, at]
            value = own.astype(F32)
            value += received[slot, :, at].astype(F32)
            for direction, step in extra:
                value += incoming[i][direction, step, :, at].astype(F32)
            store(at, value.astype(BF))
            return carry

        lax.fori_loop(0, wides[i] // WIDE_TILE, body, 0)

    def ring_copy(i, direction, step):
        cut = pieces[i] // 2
        at = pl.ds(direction * cut, cut) if step == 0 else pl.ds(0, pieces[i])
        return remote_copy(
            outgoing[i].at[direction, at],
            incoming[i].at[direction, step, at],
            ring_send.at[i, direction, step],
            ring_recv.at[i, direction, step],
            near[direction],
        )

    def ring_step(i, step):
        if step == 0:

            cut = pieces[i] // 2

            def store(at, value):
                outgoing[i][0, pl.ds(0, cut), at] = value[:cut]
                outgoing[i][1, pl.ds(cut, cut), at] = value[cut:]

            piece_sum(i, half, (), store)
            for direction in range(2):
                ring_copy(i, direction, 0).start()
            return
        for direction in range(2):
            ring_copy(i, direction, step - 1).wait()

            def store(at, value):
                outgoing[i][direction, :, at] = value

            k = half - step if direction == 0 else step - half
            piece_sum(i, k, ((direction, step - 1),), store)
            ring_copy(i, direction, step).start()

    def chip_copy(i):
        return remote_copy(
            summed.at[i - 1],
            from_chip.at[i - 1],
            chip_send.at[i],
            chip_recv.at[i],
            other_chip,
        )

    def ring_end(i):
        for direction in range(2):
            ring_copy(i, direction, half - 1).wait()

        def store(at, value):
            if i == 0:
                out_summed[:, at] = value
            else:
                summed[i - 1, :, at] = value

        piece_sum(i, 0, tuple((d, half - 1) for d in range(2)), store)
        if i > 0:
            chip_copy(i).start()
        else:
            for copy in out_copies()[:3]:
                copy.start()

    own_strip = pl.ds(pl.multiple_of(core * strip, strip), strip)

    def out_copies():
        def at(which_chip):
            return out_grad_ref.at[
                pl.ds(pl.multiple_of(core * strip + which_chip * quarter, quarter), quarter)
            ]

        done = out_summed
        return (
            pltpu.make_async_copy(done, at(chip), own_sem.at[3]),
            remote_copy(done, at(chip), chip_send.at[0], chip_recv.at[0], other_chip),
            remote_copy(done, at(chip), last_send.at[0], last_recv.at[0], other_core),
            remote_copy(at(1 - chip), at(1 - chip), last_send.at[3], last_recv.at[3], other_core),
        )

    def last_copies(i):
        src = finished.at[i - 1]
        dst = result_refs[i].at[own_strip, pl.ds(result_starts[i], wides[i])]
        return (
            pltpu.make_async_copy(src, dst, own_sem.at[3 + i]),
            remote_copy(src, dst, last_send.at[i], last_recv.at[i], other_core),
        )

    def group_end(i):
        chip_copy(i).wait()
        total = summed[i - 1].astype(F32) + from_chip[i - 1].astype(F32)
        finished[i - 1] = total.astype(BF)
        for copy in last_copies(i):
            copy.start()

    def gain_copy(k):
        return remote_copy(
            gain_terms.at[:, tile(others[k - 1], own_rows)],
            gains_in.at[k],
            gain_send.at[k - 1],
            gain_recv.at[k - 1],
            {"shard": others[k - 1]},
        )

    def gain_swap(index):
        return remote_copy(
            gain_parts.at[index],
            gain_swaps.at[index],
            swap_send.at[index],
            swap_recv.at[index],
            (other_core, other_chip)[index],
        )

    def weight_load(ref, j, wide):
        return pltpu.make_async_copy(
            ref.at[tile(j, LOAD_TILE)], weight_tile.at[j % 2, :, pl.ds(0, wide)], tile_sem.at[j % 2]
        )

    def times_transposed(left, ref, wide, store):
        blocks = width // LOAD_TILE

        def body(j, carry):
            @pl.when(j + 1 < blocks)
            def _():
                weight_load(ref, j + 1, wide).start()

            weight_load(ref, j, wide).wait()
            store(tile(j, LOAD_TILE), contract_last(left[...], weight_tile[j % 2, :, pl.ds(0, wide)]))
            return carry

        lax.fori_loop(0, blocks, body, 0)

    def turn(array):
        def body(j, carry):
            turned[tile(j), :] = array[:, tile(j)].T
            return carry

        lax.fori_loop(0, width // TILE, body, 0)

    cosine, sine = cos_ref[...], -sin_ref[...]
    wide, thin = 2 * GROUP * HEAD_SIZE, 2 * HEAD_SIZE
    key_at, value_at = width, width + key_ref.shape[1]

    def heads_pair(pair):
        allowed = allowed_rows(segc_ref[...], segr_ref[...])
        wide_at, thin_at = pl.ds(pair * wide, wide), pl.ds(pair * thin, thin)
        query, grad = query_ref[:, wide_at], grad_attended[:, wide_at]
        key, value = key_ref[:, thin_at], value_ref[:, thin_at]
        heads, keys, values = [], [], []
        for j in range(2):
            cols = slice(j * HEAD_SIZE, (j + 1) * HEAD_SIZE)
            query_rows, grad_rows = stack_heads(query, j), stack_heads(grad, j)
            probs = softmax_rows(query_rows, key[:, cols], allowed)
            grad_probs = contract_last(grad_rows, value[:, cols])
            grad_scores = (
                probs * (grad_probs - jnp.sum(probs * grad_probs, -1, keepdims=True))
            ).astype(BF)
            heads += unstack_heads(dot(grad_scores, key[:, cols]) * HEAD_SIZE ** (-0.5))
            keys.append(contract_first(grad_scores, query_rows) * HEAD_SIZE ** (-0.5))
            values.append(contract_first(probs.astype(BF), grad_rows))
        grads[:, wide_at] = rotate(jnp.concatenate(heads, 1), cosine, sine).astype(BF)
        grads[:, pl.ds(key_at + pair * thin, thin)] = rotate(
            jnp.concatenate(keys, 1), cosine, sine
        ).astype(BF)
        grads[:, pl.ds(value_at + pair * thin, thin)] = jnp.concatenate(values, 1).astype(BF)

    load_attended = pltpu.make_async_copy(attended_ref, grad_attended, own_sem.at[3])
    load_attended.start()
    own_load.start()
    for i in chains:
        for direction in range(2):
            cut = pieces[i] // 2
            blank = pl.ds((1 - direction) * cut, cut)
            incoming[i][direction, 0, blank] = jnp.zeros((cut, wides[i]), BF)

    own_load.wait()
    for copy in keep:
        copy.start()
    greet([{"shard": shard} for shard in others] + [other_core, other_chip])

    for k in range(1, count):
        for which in range(2):
            across(k, which).start()
    weight_load(out_all_ref, 0, width).start()
    load_attended.wait()
    turn(grad_attended)
    all_terms(0)
    for k in [half] + [s * j for j in range(half - 1, 0, -1) for s in (1, -1)] + [0]:
        sum_pair(k)

    def store_attended(at, value):
        grad_attended[:, at] = value.astype(BF)

    times_transposed(mid_low_ref, out_all_ref, width, store_attended)
    weight_load(qkv_all_ref, 0, grads.shape[1]).start()
    ring_step(0, 0)
    for pair in range(KEY_VALUE_HEADS // 2):
        heads_pair(pair)

    unit, scale_row = normalize(tokens_ref[...].astype(F32))
    gain = gains_ref[0:1, :]
    grad_attended[...] = (unit * gain).astype(BF)
    turn(grad_attended)
    all_terms(1)
    ring_step(1, 0)
    for copy in keep:
        copy.wait()
    for k in range(1, count):
        for which in range(2):
            across(k, which).wait_recv()
    for which in range(2):
        for index in range(2):
            group_copy(which, index).start()
    for k in range(-(half - 1), half + 1):
        core_copy(0, k).wait_send()
    all_terms(2)
    ring_step(2, 0)
    for i in in_turn:
        ring_step(i, 1)

    def store_input(at, value):
        grad_input_ref[:, at] = value

    times_transposed(grads, qkv_all_ref, grads.shape[1], store_input)
    if half > 2:
        for i in in_turn:
            ring_step(i, 2)
    unit, scale_row = normalize(tokens_ref[...].astype(F32))
    grad_normed = grad_input_ref[...]
    gain_terms[...] = jnp.zeros_like(gain_terms)
    gain_terms[0:1, :] = jnp.sum(grad_normed * unit, 0, keepdims=True)
    gain_terms[1:2, :] = gain_two_ref[...]
    for k in range(1, count):
        gain_copy(k).start()
    grad_input_ref[...] = norm_back(grad_normed * gain, unit, scale_row)
    for step in range(3, half):
        for i in in_turn:
            ring_step(i, step)
    for which in range(2):
        group_copy(which, 0).wait_recv()
        group_copy(which, 2).start()
    total = gain_terms[:, tile(me, own_rows)]
    for k in range(1, count):
        gain_copy(k).wait_recv()
        total += gains_in[k]
    gain_parts[0] = total
    gain_swap(0).start()
    for i in in_turn:
        ring_end(i)
    gain_swap(0).wait()
    gain_parts[1] = gain_parts[0] + gain_swaps[0]
    gain_swap(1).start()
    for i in (1, 2):
        group_end(i)
    out_copies()[1].wait_recv()
    out_copies()[3].start()
    gain_swap(1).wait()
    gain_grad_ref[...] = gain_parts[1] + gain_swaps[1]

    for k in range(-(half - 1), half + 1):
        pair_copy(k).wait_send()
    kept, over, passed, again = out_copies()
    kept.wait()
    over.wait_send()
    passed.wait()
    again.wait()
    for i in (1, 2):
        kept, passed = last_copies(i)
        kept.wait()
        passed.wait()
    for i in (1, 2):
        for k in range(-(half - 1), half + 1):
            core_copy(i, k).wait_send()
    for which in range(2):
        for index in range(3):
            if index > 0:
                group_copy(which, index).wait_recv()
            group_copy(which, index).wait_send()
    for k in range(1, count):
        gain_copy(k).wait_send()
        for which in range(2):
            across(k, which).wait_send()


def back(
    count,
    sums,
    mid_low,
    gain_two_term,
    attended,
    query,
    key,
    value,
    tokens,
    gains,
    tables,
    qkv_all,
    out_all,
):
    rows, width = tokens.shape
    qkv_width = qkv_all.shape[1]
    own_rows = width // count
    strip, quarter = own_rows // 2, own_rows // 4
    ff_own = sums.shape[2] // 2
    half = count // 2
    here = pl.BlockSpec(memory_space=pl.ANY)
    inside = pl.BlockSpec(memory_space=pltpu.VMEM)
    kind = jax.ShapeDtypeStruct
    dma = pltpu.SemaphoreType.DMA
    vmem = pltpu.VMEM
    return pl.pallas_call(
        functools.partial(back_kernel, count),
        in_specs=[here] + [inside] * 2 + [here] + [inside] * 9 + [here] * 2,
        out_specs=[here] * 4 + [inside] * 2,
        out_shape=[
            kind((4, quarter, count * ff_own), BF),
            kind((4, quarter, count * ff_own), BF),
            kind((own_rows, width), BF),
            kind((own_rows, qkv_width), BF),
            kind((rows, width), F32),
            kind((8, own_rows), F32),
        ],
        scratch_shapes=[
            vmem((quarter, 2 * ff_own), BF),
            vmem((width, rows), BF),
            vmem((rows, width), BF),
            vmem((rows, qkv_width), BF),
            vmem((2, LOAD_TILE, qkv_width), BF),
            vmem((count, 2, strip, width), BF),
            vmem((count, 2, strip, qkv_width // 2), BF),
            vmem((count, strip, width), BF),
            vmem((2, count, strip, qkv_width // 2), BF),
            vmem((count, quarter, width), BF),
            vmem((count, 2, quarter, width), BF),
            vmem((quarter, width), BF),
            vmem((2, quarter, width), BF),
            vmem((2, 2, strip, qkv_width // 2), BF),
            vmem((2, half, quarter, width), BF),
            vmem((2, 2, half, strip, qkv_width // 2), BF),
            vmem((2, strip, qkv_width // 2), BF),
            vmem((2, strip, qkv_width // 2), BF),
            vmem((2, strip, qkv_width // 2), BF),
            vmem((8, width), F32),
            vmem((count, 8, own_rows), F32),
            vmem((2, 8, own_rows), F32),
            vmem((2, 8, own_rows), F32),
            dma((6,)),
            dma((2,)),
            dma((2, count - 1)),
            dma((2, count - 1)),
            dma((2, 3)),
            dma((2, 3)),
            dma((3, count)),
            dma((3, count)),
            dma((3, 2, half)),
            dma((3, 2, half)),
            dma((3,)),
            dma((3,)),
            dma((4,)),
            dma((4,)),
            dma((count,)),
            dma((count,)),
            dma((count - 1,)),
            dma((count - 1,)),
            dma((2,)),
            dma((2,)),
        ],
        compiler_params=pltpu.CompilerParams(
            collective_id=2, has_side_effects=True, vmem_limit_bytes=VMEM_BYTES
        ),
        cost_estimate=pl.CostEstimate(
            flops=4 * rows * width * (qkv_width + width) + 4 * 10**9,
            bytes_accessed=60 * 10**6,
            transcendentals=2 * 10**6,
        ),
    )(
        sums,
        mid_low,
        gain_two_term,
        attended,
        query,
        key,
        value,
        tokens,
        gains,
        *tables,
        qkv_all,
        out_all,
    )


def feed_forward_parts(ring, normed_two, grad_low, w_both, w_down):
    sequence, ff_own = normed_two.shape[0], w_down.shape[0]
    low_all, normed_all = run(ring.gather(grad_low), ring.gather(normed_two))
    hidden, grad_both = {}, {}
    for k in normed_all:
        both = dot(normed_all[k], w_both)
        gate, up = both[:, :ff_own], both[:, ff_own:]
        grad_hidden = contract_last(low_all[k], w_down)
        sigmoid = jax.nn.sigmoid(gate)
        silu = gate * sigmoid
        hidden[k] = (silu * up).astype(BF)
        grad_gate = (grad_hidden * up * sigmoid * (1.0 + gate * (1.0 - sigmoid))).astype(BF)
        grad_up = (grad_hidden * silu).astype(BF)
        grad_both[k] = jnp.concatenate([grad_gate, grad_up], 1)

    def terms_of(chunks, product):
        def terms(ks):
            sources = [k if k == ring.half else -k for k in ks]
            whole = product(jnp.concatenate([chunks[k] for k in sources], 0))
            return [whole[i * sequence : (i + 1) * sequence] for i in range(len(ks))]

        return terms

    (grad_normed_two,) = run(ring.scatter(terms_of(grad_both, lambda a: contract_last(a, w_both))))
    (branch_two,) = run(ring.scatter(terms_of(hidden, lambda a: dot(a, w_down))))
    keys = list(normed_all)
    together = lambda parts: jnp.concatenate([parts[k] for k in keys], 0)
    both_term = contract_first(together(normed_all), together(grad_both))
    down_term = contract_first(together(hidden), together(low_all))
    return grad_normed_two, branch_two, both_term, down_term


def swap(array, bit):
    return lax.ppermute(array, "rep", [(i, i ^ bit) for i in range(4)])


def cols(array, start, width):
    return lax.dynamic_slice_in_dim(array, start, width, 1)


def rows_of(array, start, height):
    return lax.dynamic_slice_in_dim(array, start, height, 0)


def put(array, piece, start, axis):
    return lax.dynamic_update_slice_in_dim(array, piece, start, axis)


def gather_rows(ring, array):
    rows = array.shape[0]
    (parts,) = run(ring.gather(array))
    full = jnp.zeros((ring.count * rows, array.shape[1]), array.dtype)
    for k, part in parts.items():
        full = put(full, part, ring.at(-k) * rows, 0)
    return full


def front_parts(ring, tokens, gains_own, cotangent, tables, own, w_gate, w_up):
    count, (own_rows, wide_k) = ring.count, own[1].shape
    rep = lax.axis_index("rep")
    ff_own = w_gate.shape[1] // count
    width = tokens.shape[1]
    gains = jnp.zeros((gains_own.shape[0], width), F32)
    for k in range(count):
        piece = ring.send(gains_own, k) if k else gains_own
        gains = put(gains, piece, ring.at(-k) * own_rows, 1)
    qkv_all = gather_rows(ring, jnp.concatenate(own[:3], 1))
    out_all = gather_rows(ring, own[3])
    quarter = own_rows // 4
    gate_rows = rows_of(w_gate, rep * quarter, quarter)
    up_rows = rows_of(w_up, rep * quarter, quarter)
    sends = []
    for k in range(count):
        dest = ring.at(k) * ff_own
        piece = jnp.concatenate([cols(gate_rows, dest, ff_own), cols(up_rows, dest, ff_own)], 1)
        sends.append((piece, k))
    fetched = jnp.zeros((count, quarter, 2 * ff_own), BF)
    for k, piece in enumerate([sends[0][0]] + ring.queue(*sends[1:])):
        fetched = put(fetched, piece[None], ring.at(-k), 0)
    pieces = [fetched, swap(fetched, 2)]
    pieces += [swap(piece, 1) for piece in pieces]
    w_both = jnp.zeros((count, 4, quarter, 2 * ff_own), BF)
    for bits, piece in zip((0, 2, 1, 3), pieces):
        w_both = put(w_both, piece[:, None], rep ^ bits, 1)
    resid = tokens.astype(F32)
    unit, _ = normalize(resid)
    linear = dot((unit * gains[:1]).astype(BF), qkv_all)
    query, key, value, attended = attend(
        linear[:, :width], linear[:, width : width + wide_k], linear[:, width + wide_k :], tables
    )
    middle = resid + dot(attended, out_all)
    unit, _ = normalize(middle)
    normed_two = (unit * gains[1:2]).astype(BF)
    low = cotangent.astype(BF)
    return qkv_all, out_all, w_both, low, gains, query, key, value, attended, middle, normed_two


def back_parts(
    ring,
    both_term,
    down_term,
    mid_low,
    gain_two_term,
    attended,
    query,
    key,
    value,
    tokens,
    gains,
    tables,
    qkv_all,
    out_all,
):
    count = ring.count
    rep = lax.axis_index("rep")
    core, chip = rep % 2, rep // 2
    width = tokens.shape[1]
    own_rows = width // count
    quarter = own_rows // 4
    ff_own = both_term.shape[1] // 2
    ff = ff_own * count

    def order_halves(mine, other):
        first = core == 0
        return jnp.where(first, mine, other), jnp.where(first, other, mine)

    def sum_cores(array, half_of):
        keep, pass_on = half_of(array, core), half_of(array, 1 - core)
        return keep.astype(F32) + swap(pass_on.astype(BF), 1).astype(F32)

    both_term = both_term.reshape(count, 2, 2, quarter, 2 * ff_own)
    both_half = sum_cores(
        both_term, lambda a, c: lax.dynamic_index_in_dim(a, c, 2, keepdims=False)
    )
    keep = lax.dynamic_index_in_dim(both_half, chip, 1, keepdims=False)
    pass_on = lax.dynamic_index_in_dim(both_half, 1 - chip, 1, keepdims=False)
    both_quarter = (keep + swap(pass_on.astype(BF), 2).astype(F32)).astype(BF)
    gate_quarter = jnp.zeros((quarter, ff), BF)
    up_quarter = jnp.zeros((quarter, ff), BF)
    sends = [
        (lax.dynamic_index_in_dim(both_quarter, ring.at(k), 0, keepdims=False), k)
        for k in range(count)
    ]
    for k, piece in enumerate([sends[0][0]] + ring.queue(*sends[1:])):
        start = ring.at(-k) * ff_own
        gate_quarter = put(gate_quarter, piece[:, :ff_own], start, 1)
        up_quarter = put(up_quarter, piece[:, ff_own:], start, 1)

    def collect(quarter_rows):
        parts = [quarter_rows, swap(quarter_rows, 2)]
        parts += [swap(part, 1) for part in parts]
        full = jnp.zeros((4 * quarter, ff), BF)
        for bits, part in zip((0, 2, 1, 3), parts):
            full = put(full, part, (rep ^ bits) * quarter, 0)
        return full

    gate_grad, up_grad = collect(gate_quarter), collect(up_quarter)

    down_half = sum_cores(
        down_term, lambda a, c: rows_of(a, c * (a.shape[0] // 2), a.shape[0] // 2)
    ).astype(BF)
    down_half = (down_half.astype(F32) + swap(down_half, 2).astype(F32)).astype(BF)
    down_grad = jnp.concatenate(order_halves(down_half, swap(down_half, 1)), 0)

    def part_sums(left, grads):
        wide = grads.shape[1] // 2
        grads_mine, grads_other = cols(grads, core * wide, wide), cols(grads, (1 - core) * wide, wide)

        def terms(ks):
            blocks = [cols(left, ring.at(k) * own_rows, own_rows) for k in ks]
            block = blocks[0] if len(ks) == 1 else jnp.concatenate(blocks, 1)
            other = swap(contract_first(block, grads_other).astype(BF), 1)
            whole = contract_first(block, grads_mine) + other.astype(F32)
            return [whole[i * own_rows : (i + 1) * own_rows] for i in range(len(ks))]

        mine = run(ring.scatter(terms))[0].astype(BF)
        mine = (mine.astype(F32) + swap(mine, 2).astype(F32)).astype(BF)
        return jnp.concatenate(order_halves(mine, swap(mine, 1)), 1)

    out_grad = part_sums(attended, mid_low)
    grad_attended = contract_last(mid_low, out_all).astype(BF)
    grads = jnp.concatenate(attend_back(query, key, value, grad_attended, tables), 1)
    unit_one, scale_one = normalize(tokens.astype(F32))
    gain_one = gains[:1]
    qkv_grad = part_sums((unit_one * gain_one).astype(BF), grads)
    grad_normed_one = contract_last(grads, qkv_all)
    gain_one_term = jnp.sum(grad_normed_one * unit_one, 0, keepdims=True)
    grad_input = norm_back(grad_normed_one * gain_one, unit_one, scale_one)

    gain_terms = jnp.concatenate([gain_one_term, gain_two_term], 0)
    gain_sums = cols(gain_terms, ring.at(0) * own_rows, own_rows)
    for k in range(1, count):
        gain_sums = gain_sums + ring.send(cols(gain_terms, ring.at(k) * own_rows, own_rows), k)
    gain_sums = gain_sums + swap(gain_sums, 1)
    gain_sums = gain_sums + swap(gain_sums, 2)
    return gate_grad, up_grad, down_grad, out_grad, qkv_grad, grad_input, gain_sums


def on_device(
    count,
    tokens,
    segments,
    norm_attn,
    w_query,
    key_weight,
    value_weight,
    w_out,
    norm_mlp,
    w_gate,
    w_up,
    w_down,
    cotangent,
):
    ring = Ring(count)
    sequence, width = tokens.shape[1], tokens.shape[2]
    own_rows = w_query.shape[0]
    ff = w_gate.shape[1]
    ff_own = ff // count
    wide_k = key_weight.shape[1]
    fits = feed_forward_bytes(count, sequence, width, ff_own) <= VMEM_BYTES
    kernels = fits and sequence == own_rows == TILE

    grad_output = cotangent.reshape(sequence, width)
    cosine, sine = rope_tables(segments)
    seg_row = segments.reshape(1, sequence)
    tables = (cosine, sine, seg_row.reshape(sequence, 1), seg_row)
    own = tokens.reshape(sequence, width)
    own_weights = (w_query, key_weight, value_weight, w_out)
    gains_own = jnp.zeros((8, own_rows), F32)
    gains_own = gains_own.at[0].set(norm_attn.astype(F32)).at[1].set(norm_mlp.astype(F32))
    bring = functools.partial(front, count) if kernels else functools.partial(front_parts, ring)
    qkv_all, out_all, w_both, low, gains, query, key, value, attended, middle, normed_two = bring(
        own, gains_own, grad_output, tables, own_weights, w_gate, w_up
    )
    w_both = w_both.reshape(width, 2 * ff_own)
    gain_one, gain_two = gains[:1], gains[1:2]

    if kernels:
        grad_normed_two, branch_two, sums, down_grad = feed_forward(
            count, normed_two, low, w_both, w_down
        )
    else:
        grad_normed_two, branch_two, both_term, down_term = feed_forward_parts(
            ring, normed_two, low, w_both, w_down
        )
    output = middle + branch_two

    grad_middle, grad_mid_low, gain_two_term = middle_back(
        middle, grad_normed_two, grad_output, gain_two
    )

    if kernels:
        gate_grad, up_grad, out_grad, qkv_grad, grad_input, gain_sums = back(
            count,
            sums,
            grad_mid_low,
            gain_two_term,
            attended,
            query,
            key,
            value,
            own,
            gains,
            tables,
            qkv_all,
            out_all,
        )
    else:
        gate_grad, up_grad, down_grad, out_grad, qkv_grad, grad_input, gain_sums = back_parts(
            ring,
            both_term,
            down_term,
            grad_mid_low,
            gain_two_term,
            attended,
            query,
            key,
            value,
            own,
            gains,
            tables,
            qkv_all,
            out_all,
        )
    grad_input = grad_middle + grad_input
    qkv_grad = qkv_grad.astype(F32)

    return (
        output.reshape(tokens.shape),
        grad_input.reshape(tokens.shape),
        gain_sums[0],
        qkv_grad[:, :width],
        qkv_grad[:, width : width + wide_k],
        qkv_grad[:, width + wide_k :],
        out_grad.astype(F32),
        gain_sums[1],
        gate_grad.reshape(own_rows, ff).astype(F32),
        up_grad.reshape(own_rows, ff).astype(F32),
        down_grad.reshape(ff_own, width).astype(F32),
    )


def solution(mesh):
    row, vector, matrix = P(("shard", "rep"), None, None), P("shard"), P("shard", None)
    in_specs = (row, P(("shard", "rep"), None), vector, matrix, matrix, matrix, matrix, vector)
    in_specs += (matrix, matrix, matrix, row)
    out_specs = (row, row, vector, matrix, matrix, matrix, matrix, vector, matrix, matrix, matrix)
    return jax.shard_map(
        functools.partial(on_device, mesh.shape["shard"]),
        mesh=mesh,
        in_specs=in_specs,
        out_specs=out_specs,
        check_vma=False,
    )
```

profile of v0, /device:TPU:0, one launch (start us, length us, event | category | flops | bytes accessed | tf_op | source)
XLA Modules:
  0.0 649.3 jit_solution(3293034795220753006)
XLA Ops:
  0.7 0.7 reshape.200
  1.3 0.7 convert.12
  2.0 0.8 slice_compare_fusion
  2.9 0.3 reduce-window.6
  3.2 0.2 slice_reduce_fusion
  3.4 0.2 reduce-window.9
  3.7 1.5 copy.26.segc_ref
  5.2 0.5 fusion
  5.8 1.0 pad_maximum_fusion
  6.7 199.2 %shard_map.203 = (bf16[2048,3072]{1,0:T(8,128)(2,1)}, bf16[2048,2048]{1,0:T(8,128)(2,1)}, bf16[8,4,64,2048]{3,2,1,0:T(8,128)(2,1)}, bf16[2048,2048]{1,0:T(8,128)...) custom-call(bf16[256,2048]{1,0:T(8,128)(2,1)} %bitcast.39, ...), custom_call_target="tpu_custom_call" | custom-call | flops 7368709120 | bytes 60000000 | tf_op jit(solution)/shard_map/pallas_call | solution.py:674
  206.0 259.4 %shard_map.204 = (f32[256,2048]{1,0:T(8,128)}, f32[256,2048]{1,0:T(8,128)}, bf16[8,64,2048]{2,1,0:T(8,128)(2,1)}, bf16[4,4,64,2048]{3,2,1,0:T(8,128)(2,1)}) custom-call(bf16[256,2048]{1,0:T(8,128)(2,1)} %get-tuple-element.60.normed_ref, bf16[2048,2048]{1,0:T(8,128)(2,1)} %get-tuple-element.61.low_ref, bf16[2048,2048]{1,0:T(8,128)(2,1)} %bitcast.41, ...), custom_call_target="tpu_custom_call" | custom-call | flops 77309411328 | bytes 50000000 | tf_op jit(solution)/shard_map/pallas_call | solution.py:1161
  465.4 3.9 add_bitcast_fusion.1
  469.3 1.4 slice.63.gain_ref
  470.7 7.6 %shard_map.205 = (f32[256,2048]{1,0:T(8,128)}, bf16[256,2048]{1,0:T(8,128)(2,1)}, f32[1,2048]{1,0:T(1,128)}) custom-call(f32[256,2048]{1,0:T(8,128)} %get-tuple-element.59.middle_ref, f32[256,2048]{1,0:T(8,128)} %get-tuple-element.64.grad_ref, f32[256,2048]{1,0:T(8,128)} %bitcast.33, f32[1,2048]{1,0:T(1,128)} %slice.63.gain_ref), custom_call_target="tpu_custom_call" | custom-call | tf_op jit(solution)/shard_map/pallas_call | solution.py:1234
  478.4 146.7 %shard_map.206 = (bf16[4,64,8192]{2,1,0:T(8,128)(2,1)}, bf16[4,64,8192]{2,1,0:T(8,128)(2,1)}, bf16[256,2048]{1,0:T(8,128)(2,1)}, bf16[256,3072]{1,0:T(8,128)(2,1...) custom-call(bf16[8,64,2048]{2,1,0:T(8,128)(2,1)} %get-tuple-element.67.sums_ref, ...), custom_call_target="tpu_custom_call" | custom-call | flops 14737418240 | bytes 60000000 | tf_op jit(solution)/shard_map/pallas_call | solution.py:1748
  625.1 4.0 add_bitcast_fusion
  629.1 1.4 fusion.4
  630.4 1.1 fusion.3
  631.5 1.6 slice.69
  633.1 1.6 convert_element_type.38
  634.6 0.4 copy-done.3
  635.0 4.7 bitcast_convert_fusion.2
  639.7 4.7 bitcast_convert_fusion.1
  644.3 4.7 bitcast_convert_fusion
  (19 shorter events, 0.3 us)
Async XLA Ops:
  3.7 3.0 copy-start.5
  625.0 5.4 copy-start
  629.1 4.0 copy-start.4
  631.5 3.5 copy-start.3
  635.0 4.7 copy-start.2
  639.7 4.7 copy-start.1
where the time goes:
time: 653 us; the launch traced here: 649 us
  Pallas kernels  613 us (94%)
  other arithmetic  27.1 us (4%)
  local copies, waits for them, and re-layouts  8.28 us (1%)
    pallas_call x1, Pallas kernels, feed_forward(): pl.pallas_call(functools.partial(feed_forward_kernel, count), in_specs=[h...  259 us
    pallas_call x1, Pallas kernels, front(): pl.pallas_call(functools.partial(front_kernel, count), in_specs=[inside]...  199 us
    pallas_call x1, Pallas kernels, back(): pl.pallas_call(functools.partial(back_kernel, count), in_specs=[here] + [...  147 us

commit v1 on v0

--- a/solution.py
+++ b/solution.py
@@ -98,17 +98,22 @@
     return exponent / jnp.sum(exponent, -1, keepdims=True)
 
 
-def allowed_rows(seg_column, seg_row):
+def allowed_rows(seg_row):
     count = seg_row.shape[1]
     shape = (count, count)
-    causal = lax.broadcasted_iota(jnp.int32, shape, 0) >= lax.broadcasted_iota(jnp.int32, shape, 1)
+    at_row = lax.broadcasted_iota(jnp.int32, shape, 0)
+    at_column = lax.broadcasted_iota(jnp.int32, shape, 1)
+    causal = at_row >= at_column
+    seg_column = jnp.sum(
+        jnp.where(at_row == at_column, jnp.broadcast_to(seg_row, shape), 0), 1, keepdims=True
+    )
     one = ((seg_column == seg_row) & causal).astype(jnp.int32)
     return jnp.concatenate([one] * GROUP, 0) > 0
 
 
-def attend_kernel(q_ref, k_ref, v_ref, cos_ref, sin_ref, segc_ref, segr_ref, qo, ko, vo, ao):
+def attend_kernel(q_ref, k_ref, v_ref, cos_ref, sin_ref, segr_ref, qo, ko, vo, ao):
     cosine, sine = cos_ref[...], sin_ref[...]
-    allowed = allowed_rows(segc_ref[...], segr_ref[...])
+    allowed = allowed_rows(segr_ref[...])
     query = rotate(q_ref[...], cosine, sine).astype(BF)
     key = rotate(k_ref[...], cosine, sine).astype(BF)
     value = v_ref[...].astype(BF)
@@ -123,9 +128,9 @@
     ao[...] = jnp.concatenate(heads, 1)
 
 
-def attend_back_kernel(q_ref, k_ref, v_ref, g_ref, cos_ref, sin_ref, segc_ref, segr_ref, gq, gk, gv):
+def attend_back_kernel(q_ref, k_ref, v_ref, g_ref, cos_ref, sin_ref, segr_ref, gq, gk, gv):
     cosine, sine = cos_ref[...], -sin_ref[...]
-    allowed = allowed_rows(segc_ref[...], segr_ref[...])
+    allowed = allowed_rows(segr_ref[...])
     query, key, value, grad = q_ref[...], k_ref[...], v_ref[...], g_ref[...]
     heads, keys, values = [], [], []
     for j in range(2):
@@ -148,7 +153,7 @@
     wide = pl.BlockSpec((count, 2 * GROUP * HEAD_SIZE), lambda i: (0, i))
     thin = pl.BlockSpec((count, 2 * HEAD_SIZE), lambda i: (0, i))
     whole = lambda shape: pl.BlockSpec(shape, lambda i: (0, 0))
-    fixed = [whole((count, 128)), whole((count, 128)), whole((count, 1)), whole((1, count))]
+    fixed = [whole((count, 128)), whole((count, 128)), whole((1, count))]
     return wide, thin, fixed
 
 
@@ -304,7 +309,6 @@
     cotangent_ref,
     cos_ref,
     sin_ref,
-    segc_ref,
     segr_ref,
     query_own_ref,
     key_own_ref,
@@ -431,21 +435,18 @@
             {"shard": there},
         )
 
-    def ring_copy(i, direction, step):
+    def hops(step):
+        return ((0, 0), (0, 1), (1, 0), (1, 1)) if step < half else ((0, 0), (1, 1))
+
+    def ring_copy(i, direction, step, part):
         sign = 1 if direction == 0 else -1
-        shard = ring_shard(count, place - sign * (step - 1))
-        if step < half:
-            at = piece_of(shard, core, chip)
-        else:
-            at = piece_of(shard, core, chip, direction)
-        src = full_refs[i].at[at]
-        if step == 1:
-            src = inside[i].at[at]
+        at = piece_of(ring_shard(count, place - sign * (step - 1)), core, chip, part)
+        src = inside[i].at[at] if step == 1 else full_refs[i].at[at]
         return remote_copy(
             src,
             full_refs[i].at[at],
-            ring_send.at[i, direction, step - 1],
-            ring_recv.at[i, direction, step - 1],
+            ring_send.at[i, direction, step - 1, part],
+            ring_recv.at[i, direction, step - 1, part],
             near[direction],
         )
 
@@ -478,45 +479,42 @@
             full_refs[i].at[at], inside[i].at[at], load_sem.at[i, k + half - 1]
         )
 
-    def low_copy(direction, step):
+    def low_copy(direction, step, part):
         base = 0 if direction == 0 else half
-        to, size = (base + step) * rows, rows
-        source = to - rows
-        if step == half:
-            size = rows // 2
-            to = half * rows + direction * size
-            source = (base + half - 1) * rows + direction * size
-        src = low_all_ref.at[pl.ds(source, size)] if step > 1 else low_own
+        source = (base + step - 1) * rows if step > 1 else 0
+        to = (base + step if step < half else half) * rows
+        size = rows // 2
+        src = (low_all_ref if step > 1 else low_own).at[pl.ds(source + part * size, size)]
         return remote_copy(
             src,
-            low_all_ref.at[pl.ds(to, size)],
-            low_send.at[direction, step - 1],
-            low_recv.at[direction, step - 1],
+            low_all_ref.at[pl.ds(to + part * size, size)],
+            low_send.at[direction, step - 1, part],
+            low_recv.at[direction, step - 1, part],
             near[direction],
         )
 
-    def start_low(step):
-        for direction in range(2):
-            low_copy(direction, step).start()
+    def pass_on(copy_of, step):
+        for part, direction in hops(step):
+            copy_of(direction, step, part).wait_recv()
+            if step < half - 1 or (step == half - 1 and part == direction):
+                copy_of(direction, step + 1, part).start()
+
+    def start_low():
+        for part, direction in hops(1):
+            low_copy(direction, 1, part).start()
 
     def finish_low(step):
-        for direction in range(2):
-            low_copy(direction, step).wait_recv()
-        if step < half:
-            start_low(step + 1)
-
-    def start_step(i, step):
-        for direction in range(2):
-            ring_copy(i, direction, step).start()
+        pass_on(low_copy, step)
+
+    def start_ring(i):
+        for part, direction in hops(1):
+            ring_copy(i, direction, 1, part).start()
 
     def places(step):
         return (step, -step) if step < half else (half,)
 
     def finish_step(i, step):
-        for direction in range(2):
-            ring_copy(i, direction, step).wait_recv()
-        if step < half:
-            start_step(i, step + 1)
+        pass_on(functools.partial(ring_copy, i), step)
         for k in places(step):
             core_copy(i, k, 0).start()
 
@@ -537,7 +535,7 @@
 
     for k in range(1, count):
         gain_copy(k).start()
-    start_step(0, 1)
+    start_ring(0)
     resid = tokens_ref[...].astype(F32)
     unit, _ = normalize(resid)
     for k in range(1, count):
@@ -551,7 +549,7 @@
             for k in range(1, count):
                 for which in range(2):
                     across(k, which).start()
-    start_step(1, 1)
+    start_ring(1)
     for step in range(1, half + 1):
         pass_step(0, step)
         if step > 1:
@@ -583,7 +581,7 @@
     key_at, value_at = width, width + key_ref.shape[1]
 
     def heads_pair(pair):
-        allowed = allowed_rows(segc_ref[...], segr_ref[...])
+        allowed = allowed_rows(segr_ref[...])
         wide_at = pl.ds(pair * wide, wide)
         thin_at = pl.ds(pair * thin, thin)
         query = rotate(linear[:, wide_at], cosine, sine).astype(BF)
@@ -605,7 +603,7 @@
             finish_step(1, turn + 1)
             start_chip(1, turn + 1)
         if turn == half - 2:
-            start_low(1)
+            start_low()
         if turn < pairs:
             heads_pair(turn)
     for copy in keep:
@@ -645,12 +643,12 @@
     for copy in chip_copies + core_copies:
         copy.wait_send()
     for step in range(1, half + 1):
-        for direction in range(2):
-            low_copy(direction, step).wait_send()
+        for part, direction in hops(step):
+            low_copy(direction, step, part).wait_send()
     for i in range(2):
         for step in range(1, half + 1):
-            for direction in range(2):
-                ring_copy(i, direction, step).wait_send()
+            for part, direction in hops(step):
+                ring_copy(i, direction, step, part).wait_send()
             for k in places(step):
                 chip_copy(i, k).wait_send()
                 for which in range(2):
@@ -673,7 +671,7 @@
     dma = pltpu.SemaphoreType.DMA
     return pl.pallas_call(
         functools.partial(front_kernel, count),
-        in_specs=[inside] * 7 + [here] * 6,
+        in_specs=[inside] * 6 + [here] * 6,
         out_specs=[here] * 4 + [inside] * 7,
         out_shape=[
             kind((count * own_rows, qkv_width), BF),
@@ -699,8 +697,8 @@
             dma((2, count)),
             dma((count - 1,)),
             dma((count - 1,)),
-            dma((2, 2, half)),
-            dma((2, 2, half)),
+            dma((2, 2, half, 2)),
+            dma((2, 2, half, 2)),
             dma((2, 2, count)),
             dma((2, 2, count)),
             dma((2, count)),
@@ -709,8 +707,8 @@
             dma((2, count - 1)),
             dma((3,)),
             dma((3,)),
-            dma((2, half)),
-            dma((2, half)),
+            dma((2, half, 2)),
+            dma((2, half, 2)),
         ],
         compiler_params=pltpu.CompilerParams(
             collective_id=1, has_side_effects=True, vmem_limit_bytes=VMEM_BYTES
@@ -1209,10 +1207,14 @@
     )(normed, low, w_both, w_down)
 
 
-def middle_back_kernel(middle_ref, grad_ref, cotangent_ref, gain_ref, out_ref, low_ref, term_ref):
-    unit, scale_row = normalize(middle_ref[...])
+def middle_back_kernel(
+    middle_ref, branch_ref, grad_ref, cotangent_ref, gains_ref, result_ref, out_ref, low_ref, term_ref
+):
+    middle = middle_ref[...]
+    result_ref[...] = middle + branch_ref[...]
+    unit, scale_row = normalize(middle)
     grad = grad_ref[...]
-    total = cotangent_ref[...] + norm_back(grad * gain_ref[...], unit, scale_row)
+    total = cotangent_ref[...] + norm_back(grad * gains_ref[1:2, :], unit, scale_row)
     out_ref[...] = total
     low_ref[...] = total.astype(BF)
     term = jnp.sum(grad * unit, 0, keepdims=True)
@@ -1226,18 +1228,20 @@
         term_ref[...] += term
 
 
-def middle_back(middle, grad, cotangent, gain):
+def middle_back(middle, branch, grad, cotangent, gains):
     rows, width = middle.shape
-    block = pl.BlockSpec((rows // 8, width), lambda i: (i, 0))
+    block = pl.BlockSpec((rows // 4, width), lambda i: (i, 0))
     fixed = pl.BlockSpec((1, width), lambda i: (0, 0))
     kind = jax.ShapeDtypeStruct
+    full = kind((rows, width), F32)
     return pl.pallas_call(
         middle_back_kernel,
-        grid=(8,),
-        in_specs=[block, block, block, fixed],
-        out_specs=[block, block, fixed],
-        out_shape=[kind((rows, width), F32), kind((rows, width), BF), kind((1, width), F32)],
-    )(middle, grad, cotangent, gain)
+        grid=(4,),
+        in_specs=[block] * 4 + [pl.BlockSpec(gains.shape, lambda i: (0, 0))],
+        out_specs=[block] * 3 + [fixed],
+        out_shape=[full, full, kind((rows, width), BF), kind((1, width), F32)],
+        compiler_params=pltpu.CompilerParams(vmem_limit_bytes=VMEM_BYTES),
+    )(middle, branch, grad, cotangent, gains)
 
 
 def back_kernel(
@@ -1253,7 +1257,6 @@
     gains_ref,
     cos_ref,
     sin_ref,
-    segc_ref,
     segr_ref,
     qkv_all_ref,
     out_all_ref,
@@ -1579,7 +1582,7 @@
     key_at, value_at = width, width + key_ref.shape[1]
 
     def heads_pair(pair):
-        allowed = allowed_rows(segc_ref[...], segr_ref[...])
+        allowed = allowed_rows(segr_ref[...])
         wide_at, thin_at = pl.ds(pair * wide, wide), pl.ds(pair * thin, thin)
         query, grad = query_ref[:, wide_at], grad_attended[:, wide_at]
         key, value = key_ref[:, thin_at], value_ref[:, thin_at]
@@ -1747,7 +1750,7 @@
     vmem = pltpu.VMEM
     return pl.pallas_call(
         functools.partial(back_kernel, count),
-        in_specs=[here] + [inside] * 2 + [here] + [inside] * 9 + [here] * 2,
+        in_specs=[here] + [inside] * 2 + [here] + [inside] * 8 + [here] * 2,
         out_specs=[here] * 4 + [inside] * 2,
         out_shape=[
             kind((4, quarter, count * ff_own), BF),
@@ -1826,6 +1829,36 @@
     )
 
 
+def results_kernel(*refs):
+    gate, up, down, out, qkv, middle, change = refs[:7]
+    gate_to, up_to, down_to, out_to, query_to, key_to, value_to, input_to = refs[7:]
+    for source, result in ((gate, gate_to), (up, up_to), (down, down_to), (out, out_to)):
+        result[...] = source[...].astype(F32)
+    start = 0
+    for result in (query_to, key_to, value_to):
+        result[...] = qkv[:, start : start + result.shape[1]].astype(F32)
+        start += result.shape[1]
+    input_to[...] = middle[...] + change[...]
+
+
+def results(gate, up, down, out, qkv, wide_k, grad_middle, change):
+    steps = 8
+    kind = jax.ShapeDtypeStruct
+    sources = (gate, up, down, out, qkv, grad_middle, change)
+    width = out.shape[1]
+    shapes = [a.shape for a in (gate, up, down, out)]
+    shapes += [(qkv.shape[0], w) for w in (width, wide_k, wide_k)] + [change.shape]
+    block = lambda shape: pl.BlockSpec((shape[0] // steps, shape[1]), lambda i: (i, 0))
+    return pl.pallas_call(
+        results_kernel,
+        grid=(steps,),
+        in_specs=[block(a.shape) for a in sources],
+        out_specs=[block(shape) for shape in shapes],
+        out_shape=[kind(shape, F32) for shape in shapes],
+        compiler_params=pltpu.CompilerParams(vmem_limit_bytes=VMEM_BYTES),
+    )(*sources)
+
+
 def feed_forward_parts(ring, normed_two, grad_low, w_both, w_down):
     sequence, ff_own = normed_two.shape[0], w_down.shape[0]
     low_all, normed_all = run(ring.gather(grad_low), ring.gather(normed_two))
@@ -2050,8 +2083,7 @@
 
     grad_output = cotangent.reshape(sequence, width)
     cosine, sine = rope_tables(segments)
-    seg_row = segments.reshape(1, sequence)
-    tables = (cosine, sine, seg_row.reshape(sequence, 1), seg_row)
+    tables = (cosine, sine, segments.reshape(1, sequence))
     own = tokens.reshape(sequence, width)
     own_weights = (w_query, key_weight, value_weight, w_out)
     gains_own = jnp.zeros((8, own_rows), F32)
@@ -2061,7 +2093,6 @@
         own, gains_own, grad_output, tables, own_weights, w_gate, w_up
     )
     w_both = w_both.reshape(width, 2 * ff_own)
-    gain_one, gain_two = gains[:1], gains[1:2]
 
     if kernels:
         grad_normed_two, branch_two, sums, down_grad = feed_forward(
@@ -2071,10 +2102,8 @@
         grad_normed_two, branch_two, both_term, down_term = feed_forward_parts(
             ring, normed_two, low, w_both, w_down
         )
-    output = middle + branch_two
-
-    grad_middle, grad_mid_low, gain_two_term = middle_back(
-        middle, grad_normed_two, grad_output, gain_two
+    output, grad_middle, grad_mid_low, gain_two_term = middle_back(
+        middle, branch_two, grad_normed_two, grad_output, gains
     )
 
     if kernels:
@@ -2110,21 +2139,29 @@
             qkv_all,
             out_all,
         )
-    grad_input = grad_middle + grad_input
-    qkv_grad = qkv_grad.astype(F32)
+    gate_grad, up_grad, down_grad, out_grad, query_grad, key_grad, value_grad, grad_input = results(
+        gate_grad.reshape(own_rows, ff),
+        up_grad.reshape(own_rows, ff),
+        down_grad.reshape(ff_own, width),
+        out_grad,
+        qkv_grad,
+        wide_k,
+        grad_middle,
+        grad_input,
+    )
 
     return (
         output.reshape(tokens.shape),
         grad_input.reshape(tokens.shape),
         gain_sums[0],
-        qkv_grad[:, :width],
-        qkv_grad[:, width : width + wide_k],
-        qkv_grad[:, width + wide_k :],
-        out_grad.astype(F32),
+        query_grad,
+        key_grad,
+        value_grad,
+        out_grad,
         gain_sums[1],
-        gate_grad.reshape(own_rows, ff).astype(F32),
-        up_grad.reshape(own_rows, ff).astype(F32),
-        down_grad.reshape(ff_own, width).astype(F32),
+        gate_grad,
+        up_grad,
+        down_grad,
     )
 
 

time: 653 us -> 640 us (0.980)
  other arithmetic: 27.1 us -> 3.61 us
  Pallas kernels: 613 us -> 630 us
    pallas_call x1 -> x2, Pallas kernels: 7.63 us -> 25.2 us  [the longest x1 18.5 us: results(): pl.pallas_call(results_kernel, grid=(steps,), in_specs=[block(a.shape) fo...]
    convert_element_type x4 -> x0, other arithmetic: 15.6 us -> none  [the longest x1 4.75 us: on_device(): down_grad.reshape(ff_own, width).astype(F32)]
    reshape x2 -> x0, other arithmetic: 7.88 us -> none  [the longest x1 4 us: on_device(): grad_input.reshape(tokens.shape)]
where the time goes in v1:
time: 640 us; the launch traced here: 637 us
  Pallas kernels  630 us (98%)
    pallas_call x1, Pallas kernels, feed_forward(): pl.pallas_call(functools.partial(feed_forward_kernel, count), in_specs=[h...  260 us
    pallas_call x1, Pallas kernels, front(): pl.pallas_call(functools.partial(front_kernel, count), in_specs=[inside]...  198 us
    pallas_call x1, Pallas kernels, back(): pl.pallas_call(functools.partial(back_kernel, count), in_specs=[here] + [...  148 us
    pallas_call x1, Pallas kernels, results(): pl.pallas_call(results_kernel, grid=(steps,), in_specs=[block(a.shape) fo...  18.5 us

profile of v1, /device:TPU:0, one launch (start us, length us, event | category | flops | bytes accessed | tf_op | source)
XLA Modules:
  0.0 637.1 jit_solution(18326465185007789497)
XLA Ops:
  0.7 0.7 reshape.197
  1.3 0.7 convert.9
  2.0 0.8 slice_compare_fusion
  2.8 0.1 compare_reduce_fusion
  2.9 0.3 reduce-window.6
  3.2 0.2 slice_reduce_fusion
  3.4 0.2 reduce-window.9
  3.6 0.1 broadcast.79
  3.7 0.0 copy-start
  3.7 0.5 fusion
  4.3 1.0 pad_maximum_fusion
  5.3 0.0 copy-done
  5.3 197.8 %shard_map.203 = (bf16[2048,3072]{1,0:T(8,128)(2,1)}, bf16[2048,2048]{1,0:T(8,128)(2,1)}, bf16[8,4,64,2048]{3,2,1,0:T(8,128)(2,1)}, bf16[2048,2048]{1,0:T(8,128)...) custom-call(bf16[256,2048]{1,0:T(8,128)(2,1)} %bitcast.34, ...), custom_call_target="tpu_custom_call" | custom-call | flops 7368709120 | bytes 60000000 | tf_op jit(solution)/shard_map/pallas_call | solution.py:672
  203.1 259.7 %shard_map.204 = (f32[256,2048]{1,0:T(8,128)}, f32[256,2048]{1,0:T(8,128)}, bf16[8,64,2048]{2,1,0:T(8,128)(2,1)}, bf16[4,4,64,2048]{3,2,1,0:T(8,128)(2,1)}) custom-call(bf16[256,2048]{1,0:T(8,128)(2,1)} %get-tuple-element.69.normed_ref, bf16[2048,2048]{1,0:T(8,128)(2,1)} %get-tuple-element.70.low_ref, bf16[2048,2048]{1,0:T(8,128)(2,1)} %bitcast.36, ...), custom_call_target="tpu_custom_call" | custom-call | flops 77309411328 | bytes 50000000 | tf_op jit(solution)/shard_map/pallas_call | solution.py:1159
  462.8 6.7 %shard_map.205 = (f32[256,2048]{1,0:T(8,128)}, f32[256,2048]{1,0:T(8,128)}, bf16[256,2048]{1,0:T(8,128)(2,1)}, f32[1,2048]{1,0:T(1,128)}) custom-call(f32[256,2048]{1,0:T(8,128)} %get-tuple-element.68.middle_ref, f32[256,2048]{1,0:T(8,128)} %get-tuple-element.72.branch_ref, f32[256,2048]{1,0:T(8,128)} %get-tuple-element.73.grad_ref, f32[256,2048]{1,0:T(8,128)} %bitcast.27, ...), custom_call_target="tpu_custom_call" | custom-call | tf_op jit(solution)/shard_map/pallas_call | solution.py:1237
  469.5 147.5 %shard_map.206 = (bf16[4,64,8192]{2,1,0:T(8,128)(2,1)}, bf16[4,64,8192]{2,1,0:T(8,128)(2,1)}, bf16[256,2048]{1,0:T(8,128)(2,1)}, bf16[256,3072]{1,0:T(8,128)(2,1...) custom-call(bf16[8,64,2048]{2,1,0:T(8,128)(2,1)} %get-tuple-element.76.sums_ref, ...), custom_call_target="tpu_custom_call" | custom-call | flops 14737418240 | bytes 60000000 | tf_op jit(solution)/shard_map/pallas_call | solution.py:1751
  617.0 1.3 fusion.3
  618.3 18.5 %shard_map.207 = (f32[256,8192]{1,0:T(8,128)}, f32[256,8192]{1,0:T(8,128)}, f32[1024,2048]{1,0:T(8,128)}, f32[256,2048]{1,0:T(8,128)}, f32[256,2048]{1,0:T(8,128...) custom-call(bf16[256,8192]{1,0:T(8,128)(2,1)} %bitcast.24, bf16[256,8192]{1,0:T(8,128)(2,1)} %bitcast.25, ...), custom_call_target="tpu_custom_call" | custom-call | tf_op jit(solution)/shard_map/pallas_call | solution.py:1852
  (6 shorter events, 0.1 us)
Async XLA Ops:
  3.7 1.5 copy-start

commit v2 on v1

--- a/solution.py
+++ b/solution.py
@@ -899,7 +899,7 @@
         )
 
     units = (width + ff) // TILE
-    per_step = -(-(units + 3) // (half - 1))
+    per_step = -(-(units + 3) // (half - 1)) + 1
     quarter = TILE // 4
 
     def core_copy(unit):

time: 640 us -> 638 us (level)
  no operation moved by 1% of the time
where the time goes in v2:
time: 638 us; the launch traced here: 635 us
  Pallas kernels  628 us (98%)
    pallas_call x1, Pallas kernels, feed_forward(): pl.pallas_call(functools.partial(feed_forward_kernel, count), in_specs=[h...  259 us
    pallas_call x1, Pallas kernels, front(): pl.pallas_call(functools.partial(front_kernel, count), in_specs=[inside]...  198 us
    pallas_call x1, Pallas kernels, back(): pl.pallas_call(functools.partial(back_kernel, count), in_specs=[here] + [...  146 us
    pallas_call x1, Pallas kernels, results(): pl.pallas_call(results_kernel, grid=(steps,), in_specs=[block(a.shape) fo...  18.5 us

profile of v2, /device:TPU:0, one launch (start us, length us, event | category | flops | bytes accessed | tf_op | source)
XLA Modules:
  0.0 634.9 jit_solution(14226776060450124460)
XLA Ops:
  0.7 0.7 reshape.197
  1.3 0.7 convert.9
  2.0 0.8 slice_compare_fusion
  2.8 0.1 compare_reduce_fusion
  2.9 0.3 reduce-window.6
  3.2 0.2 slice_reduce_fusion
  3.4 0.2 reduce-window.9
  3.6 0.1 broadcast.79
  3.7 0.0 copy-start
  3.7 0.5 fusion
  4.3 1.0 pad_maximum_fusion
  5.3 0.0 copy-done
  5.3 197.8 %shard_map.203 = (bf16[2048,3072]{1,0:T(8,128)(2,1)}, bf16[2048,2048]{1,0:T(8,128)(2,1)}, bf16[8,4,64,2048]{3,2,1,0:T(8,128)(2,1)}, bf16[2048,2048]{1,0:T(8,128)...) custom-call(bf16[256,2048]{1,0:T(8,128)(2,1)} %bitcast.34, ...), custom_call_target="tpu_custom_call" | custom-call | flops 7368709120 | bytes 60000000 | tf_op jit(solution)/shard_map/pallas_call | solution.py:672
  203.1 259.0 %shard_map.204 = (f32[256,2048]{1,0:T(8,128)}, f32[256,2048]{1,0:T(8,128)}, bf16[8,64,2048]{2,1,0:T(8,128)(2,1)}, bf16[4,4,64,2048]{3,2,1,0:T(8,128)(2,1)}) custom-call(bf16[256,2048]{1,0:T(8,128)(2,1)} %get-tuple-element.69.normed_ref, bf16[2048,2048]{1,0:T(8,128)(2,1)} %get-tuple-element.70.low_ref, bf16[2048,2048]{1,0:T(8,128)(2,1)} %bitcast.36, ...), custom_call_target="tpu_custom_call" | custom-call | flops 77309411328 | bytes 50000000 | tf_op jit(solution)/shard_map/pallas_call | solution.py:1159
  462.1 6.7 %shard_map.205 = (f32[256,2048]{1,0:T(8,128)}, f32[256,2048]{1,0:T(8,128)}, bf16[256,2048]{1,0:T(8,128)(2,1)}, f32[1,2048]{1,0:T(1,128)}) custom-call(f32[256,2048]{1,0:T(8,128)} %get-tuple-element.68.middle_ref, f32[256,2048]{1,0:T(8,128)} %get-tuple-element.72.branch_ref, f32[256,2048]{1,0:T(8,128)} %get-tuple-element.73.grad_ref, f32[256,2048]{1,0:T(8,128)} %bitcast.27, ...), custom_call_target="tpu_custom_call" | custom-call | tf_op jit(solution)/shard_map/pallas_call | solution.py:1237
  468.8 146.0 %shard_map.206 = (bf16[4,64,8192]{2,1,0:T(8,128)(2,1)}, bf16[4,64,8192]{2,1,0:T(8,128)(2,1)}, bf16[256,2048]{1,0:T(8,128)(2,1)}, bf16[256,3072]{1,0:T(8,128)(2,1...) custom-call(bf16[8,64,2048]{2,1,0:T(8,128)(2,1)} %get-tuple-element.76.sums_ref, ...), custom_call_target="tpu_custom_call" | custom-call | flops 14737418240 | bytes 60000000 | tf_op jit(solution)/shard_map/pallas_call | solution.py:1751
  614.8 1.3 fusion.3
  616.1 18.5 %shard_map.207 = (f32[256,8192]{1,0:T(8,128)}, f32[256,8192]{1,0:T(8,128)}, f32[1024,2048]{1,0:T(8,128)}, f32[256,2048]{1,0:T(8,128)}, f32[256,2048]{1,0:T(8,128...) custom-call(bf16[256,8192]{1,0:T(8,128)(2,1)} %bitcast.24, bf16[256,8192]{1,0:T(8,128)(2,1)} %bitcast.25, ...), custom_call_target="tpu_custom_call" | custom-call | tf_op jit(solution)/shard_map/pallas_call | solution.py:1852
  (6 shorter events, 0.1 us)
Async XLA Ops:
  3.7 1.5 copy-start

commit v3 on v2

--- a/solution.py
+++ b/solution.py
@@ -899,7 +899,7 @@
         )
 
     units = (width + ff) // TILE
-    per_step = -(-(units + 3) // (half - 1)) + 1
+    per_step = -(-(units + 3) // (half - 1)) + 2
     quarter = TILE // 4
 
     def core_copy(unit):

time: 638 us -> 642 us (level)
  no operation moved by 1% of the time
where the time goes in v3:
time: 642 us; the launch traced here: 639 us
  Pallas kernels  632 us (98%)
    pallas_call x1, Pallas kernels, feed_forward(): pl.pallas_call(functools.partial(feed_forward_kernel, count), in_specs=[h...  262 us
    pallas_call x1, Pallas kernels, front(): pl.pallas_call(functools.partial(front_kernel, count), in_specs=[inside]...  198 us
    pallas_call x1, Pallas kernels, back(): pl.pallas_call(functools.partial(back_kernel, count), in_specs=[here] + [...  147 us
    pallas_call x1, Pallas kernels, results(): pl.pallas_call(results_kernel, grid=(steps,), in_specs=[block(a.shape) fo...  18.5 us

profile of v3, /device:TPU:0, one launch (start us, length us, event | category | flops | bytes accessed | tf_op | source)
XLA Modules:
  0.0 638.8 jit_solution(14490999277491893131)
XLA Ops:
  0.7 0.7 reshape.197
  1.3 0.7 convert.9
  2.0 0.8 slice_compare_fusion
  2.8 0.1 compare_reduce_fusion
  2.9 0.3 reduce-window.6
  3.2 0.2 slice_reduce_fusion
  3.4 0.2 reduce-window.9
  3.6 0.1 broadcast.79
  3.7 0.0 copy-start
  3.7 0.5 fusion
  4.3 1.0 pad_maximum_fusion
  5.3 0.0 copy-done
  5.3 197.8 %shard_map.203 = (bf16[2048,3072]{1,0:T(8,128)(2,1)}, bf16[2048,2048]{1,0:T(8,128)(2,1)}, bf16[8,4,64,2048]{3,2,1,0:T(8,128)(2,1)}, bf16[2048,2048]{1,0:T(8,128)...) custom-call(bf16[256,2048]{1,0:T(8,128)(2,1)} %bitcast.34, ...), custom_call_target="tpu_custom_call" | custom-call | flops 7368709120 | bytes 60000000 | tf_op jit(solution)/shard_map/pallas_call | solution.py:672
  203.1 261.7 %shard_map.204 = (f32[256,2048]{1,0:T(8,128)}, f32[256,2048]{1,0:T(8,128)}, bf16[8,64,2048]{2,1,0:T(8,128)(2,1)}, bf16[4,4,64,2048]{3,2,1,0:T(8,128)(2,1)}) custom-call(bf16[256,2048]{1,0:T(8,128)(2,1)} %get-tuple-element.69.normed_ref, bf16[2048,2048]{1,0:T(8,128)(2,1)} %get-tuple-element.70.low_ref, bf16[2048,2048]{1,0:T(8,128)(2,1)} %bitcast.36, ...), custom_call_target="tpu_custom_call" | custom-call | flops 77309411328 | bytes 50000000 | tf_op jit(solution)/shard_map/pallas_call | solution.py:1159
  464.7 6.7 %shard_map.205 = (f32[256,2048]{1,0:T(8,128)}, f32[256,2048]{1,0:T(8,128)}, bf16[256,2048]{1,0:T(8,128)(2,1)}, f32[1,2048]{1,0:T(1,128)}) custom-call(f32[256,2048]{1,0:T(8,128)} %get-tuple-element.68.middle_ref, f32[256,2048]{1,0:T(8,128)} %get-tuple-element.72.branch_ref, f32[256,2048]{1,0:T(8,128)} %get-tuple-element.73.grad_ref, f32[256,2048]{1,0:T(8,128)} %bitcast.27, ...), custom_call_target="tpu_custom_call" | custom-call | tf_op jit(solution)/shard_map/pallas_call | solution.py:1237
  471.5 147.2 %shard_map.206 = (bf16[4,64,8192]{2,1,0:T(8,128)(2,1)}, bf16[4,64,8192]{2,1,0:T(8,128)(2,1)}, bf16[256,2048]{1,0:T(8,128)(2,1)}, bf16[256,3072]{1,0:T(8,128)(2,1...) custom-call(bf16[8,64,2048]{2,1,0:T(8,128)(2,1)} %get-tuple-element.76.sums_ref, ...), custom_call_target="tpu_custom_call" | custom-call | flops 14737418240 | bytes 60000000 | tf_op jit(solution)/shard_map/pallas_call | solution.py:1751
  618.7 1.3 fusion.3
  620.0 18.5 %shard_map.207 = (f32[256,8192]{1,0:T(8,128)}, f32[256,8192]{1,0:T(8,128)}, f32[1024,2048]{1,0:T(8,128)}, f32[256,2048]{1,0:T(8,128)}, f32[256,2048]{1,0:T(8,128...) custom-call(bf16[256,8192]{1,0:T(8,128)(2,1)} %bitcast.24, bf16[256,8192]{1,0:T(8,128)(2,1)} %bitcast.25, ...), custom_call_target="tpu_custom_call" | custom-call | tf_op jit(solution)/shard_map/pallas_call | solution.py:1852
  (6 shorter events, 0.1 us)
Async XLA Ops:
  3.7 1.5 copy-start
